TPU v7x, 32 devices: a whole 2x2x4 slice. The times are simulated.
32 devices in a mesh: batch: 16 (over z, y, core), blk: 2 (over x).
Axes of the slice: x: 2, y: 2, z: 4, core: 2. Of those that a mesh axis runs over, the one named last changes fastest.
Arguments:
- tokens: bfloat16 [128, 512, 768], P('batch', 'blk'), may hold values from -6 to 6
- span_mask: int32 [128, 512], P('batch', 'blk'), may hold values from 0 to 1, as said below
- cotangent: bfloat16 [128, 512, 768], P('batch', 'blk'), may hold values from -6 to 6
- w_query: bfloat16 [768, 768], P('batch'), may hold values from -0.21875 to 0.21875
- b_query: bfloat16 [768], P('batch'), may hold values from -3 to 3
- w_key: bfloat16 [768, 768], P('batch'), may hold values from -0.21875 to 0.21875
- w_value: bfloat16 [768, 768], P('batch'), may hold values from -0.21875 to 0.21875
- b_value: bfloat16 [768], P('batch'), may hold values from -0.19921875 to 0.19921875
- w_out: bfloat16 [768, 768], P('batch'), may hold values from -2.5 to 2.5
- b_out: bfloat16 [768], P('batch'), may hold values from -2 to 2
- gain_first: bfloat16 [768], P('batch'), may hold values from 0.25 to 1.75
- bias_first: bfloat16 [768], P('batch'), may hold values from -2 to 2
- w_inner: bfloat16 [768, 3072], P('batch'), may hold values from -0.21875 to 0.21875
- b_inner: bfloat16 [3072], P('batch'), may hold values from -2 to 2
- w_outer: bfloat16 [3072, 768], P('batch'), may hold values from -0.109375 to 0.109375
- b_outer: bfloat16 [768], P('batch'), may hold values from -2 to 2
- gain_second: bfloat16 [768], P('batch'), may hold values from 0.25 to 1.75
- bias_second: bfloat16 [768], P('batch'), may hold values from -2 to 2
Outputs:
- output: bfloat16 [128, 512, 768], P('batch', 'blk')
- grad_tokens: bfloat16 [128, 512, 768], P('batch', 'blk')
- grad_w_query: float32 [768, 768], P('batch')
- grad_b_query: float32 [768], P('batch')
- grad_w_key: float32 [768, 768], P('batch')
- grad_w_value: float32 [768, 768], P('batch')
- grad_b_value: float32 [768], P('batch')
- grad_w_out: float32 [768, 768], P('batch')
- grad_b_out: float32 [768], P('batch')
- grad_gain_first: float32 [768], P('batch')
- grad_bias_first: float32 [768], P('batch')
- grad_w_inner: float32 [768, 3072], P('batch')
- grad_b_inner: float32 [3072], P('batch')
- grad_w_outer: float32 [3072, 768], P('batch')
- grad_b_outer: float32 [768], P('batch')
- grad_gain_second: float32 [768], P('batch')
- grad_bias_second: float32 [768], P('batch')
Inputs may be any that keep to these rules, and one draw needn't show every extreme that they name: `span_mask`: masked positions come in runs of 6 or more consecutive tokens, except where a run is cut by the end of the sequence; the masked share differs from sequence to sequence.
All inputs are finite; a program needn't handle non-finite values.
Results may differ from a plain program's by a relative error of at most 0.04.
Values may be sent and summed in bfloat16 or wider, within the bound.
A program may use at most 512 MiB of HBM per device.

v0:
```python
import jax
import jax.numpy as jnp
from jax import lax
from jax.sharding import PartitionSpec as P

HEADS = 12
HEAD_DIM = 64


epsilon = 1e-06


def layer_norm(values, gain, bias):
    center = values - jnp.mean(values, -1, keepdims=True)
    inverse = lax.rsqrt(jnp.mean(center * center, -1, keepdims=True) + epsilon)
    normed = center * inverse
    return (normed * gain.astype(jnp.float32) + bias.astype(jnp.float32), normed, inverse)


def norm_back(grad, normed, inverse, gain):
    scaled = grad * gain.astype(jnp.float32)
    return inverse * (
        scaled
        - jnp.mean(scaled, -1, keepdims=True)
        - normed * jnp.mean(scaled * normed, -1, keepdims=True)
    )


def weight_grad(left, right):
    return lax.dot_general(
        left, right, (((0,), (0,)), ((), ())), preferred_element_type=jnp.float32
    )


def back_product(grad, matrix):
    return lax.dot_general(
        grad, matrix, (((1,), (1,)), ((), ())), preferred_element_type=jnp.float32
    )


def column_sum(values):
    return jnp.sum(values.astype(jnp.float32), 0)


def score_grads(query_heads, keys_piece, values_piece, grad_context, log_total, delta, score_scale):
    scores = (
        jnp.einsum("rqhd,rkhd->rhqk", query_heads, keys_piece, preferred_element_type=jnp.float32)
        * score_scale
    )
    probs = jnp.exp(scores - log_total[..., None])
    grad_probs = jnp.einsum(
        "rqhd,rkhd->rhqk", grad_context, values_piece, preferred_element_type=jnp.float32
    )
    grad_scores = (probs * (grad_probs - delta[..., None])).astype(jnp.bfloat16)
    return (probs, grad_scores)


def body(
    tokens,
    span_mask,
    cotangent,
    w_query,
    b_query,
    w_key,
    w_value,
    b_value,
    w_out,
    b_out,
    gain_first,
    bias_first,
    w_inner,
    b_inner,
    w_outer,
    b_outer,
    gain_second,
    bias_second,
):
    (
        w_query,
        b_query,
        w_key,
        w_value,
        b_value,
        w_out,
        b_out,
        gain_first,
        bias_first,
        w_inner,
        b_inner,
        w_outer,
        b_outer,
        gain_second,
        bias_second,
    ) = (
        lax.all_gather(w_query, "batch", axis=0, tiled=True),
        lax.all_gather(b_query, "batch", axis=0, tiled=True),
        lax.all_gather(w_key, "batch", axis=0, tiled=True),
        lax.all_gather(w_value, "batch", axis=0, tiled=True),
        lax.all_gather(b_value, "batch", axis=0, tiled=True),
        lax.all_gather(w_out, "batch", axis=0, tiled=True),
        lax.all_gather(b_out, "batch", axis=0, tiled=True),
        lax.all_gather(gain_first, "batch", axis=0, tiled=True),
        lax.all_gather(bias_first, "batch", axis=0, tiled=True),
        lax.all_gather(w_inner, "batch", axis=0, tiled=True),
        lax.all_gather(b_inner, "batch", axis=0, tiled=True),
        lax.all_gather(w_outer, "batch", axis=0, tiled=True),
        lax.all_gather(b_outer, "batch", axis=0, tiled=True),
        lax.all_gather(gain_second, "batch", axis=0, tiled=True),
        lax.all_gather(bias_second, "batch", axis=0, tiled=True),
    )
    rows, stretch, width = tokens.shape
    heads = HEADS
    depth = width // heads
    score_scale = HEAD_DIM ** (-0.5)
    flat = tokens.reshape(rows * stretch, width)
    queries = (
        jnp.dot(flat, w_query, preferred_element_type=jnp.float32) + b_query.astype(jnp.float32)
    ).astype(jnp.bfloat16)
    keys_own = jnp.dot(flat, w_key, preferred_element_type=jnp.float32).astype(jnp.bfloat16)
    values_own = (
        jnp.dot(flat, w_value, preferred_element_type=jnp.float32) + b_value.astype(jnp.float32)
    ).astype(jnp.bfloat16)
    query_heads = queries.reshape(rows, stretch, heads, depth)
    keys_own = keys_own.reshape(rows, stretch, width)
    values_own = values_own.reshape(rows, stretch, width)
    pieces = (
        lax.all_gather(keys_own, "blk", axis=1, tiled=True),
        lax.all_gather(values_own, "blk", axis=1, tiled=True),
    )
    best = jnp.full((rows, heads, stretch), -1e30, jnp.float32)
    keys_piece = pieces[0].reshape(rows, -1, heads, depth)
    values_piece = pieces[1].reshape(rows, -1, heads, depth)
    scores = (
        jnp.einsum("rqhd,rkhd->rhqk", query_heads, keys_piece, preferred_element_type=jnp.float32)
        * score_scale
    )
    newest = jnp.maximum(best, jnp.max(scores, -1))
    weights = jnp.exp(scores - newest[..., None])
    total = jnp.sum(weights, -1)
    accum = jnp.einsum(
        "rhqk,rkhd->rhqd",
        weights.astype(jnp.bfloat16),
        values_piece,
        preferred_element_type=jnp.float32,
    )
    best, total, accum = (newest, total, accum)
    context = accum / total[..., None]
    log_total = best + jnp.log(total)
    context_low = context.transpose(0, 2, 1, 3).reshape(rows * stretch, width).astype(jnp.bfloat16)
    branch = jnp.dot(context_low, w_out, preferred_element_type=jnp.float32) + b_out.astype(
        jnp.float32
    )
    middle, normed_first, inverse_first = layer_norm(
        flat.astype(jnp.float32) + branch, gain_first, bias_first
    )
    middle_low = middle.astype(jnp.bfloat16)
    inner = jnp.dot(middle_low, w_inner, preferred_element_type=jnp.float32) + b_inner.astype(
        jnp.float32
    )
    activated, gelu_back = jax.vjp(lambda value: jax.nn.gelu(value, approximate=False), inner)
    activated_low = activated.astype(jnp.bfloat16)
    second_sum = (
        middle
        + jnp.dot(activated_low, w_outer, preferred_element_type=jnp.float32)
        + b_outer.astype(jnp.float32)
    )
    result, normed_second, inverse_second = layer_norm(second_sum, gain_second, bias_second)
    output = result.astype(jnp.bfloat16).reshape(rows, stretch, width)
    grad_result = cotangent.reshape(rows * stretch, width).astype(jnp.float32) * span_mask.reshape(
        rows * stretch, 1
    ).astype(jnp.float32)
    grad_gain_second = jnp.sum(grad_result * normed_second, 0)
    grad_bias_second = jnp.sum(grad_result, 0)
    grad_second = norm_back(grad_result, normed_second, inverse_second, gain_second)
    grad_ffn = grad_second.astype(jnp.bfloat16)
    grad_w_outer = weight_grad(activated_low, grad_ffn)
    grad_b_outer = column_sum(grad_ffn)
    grad_inner = gelu_back(back_product(grad_ffn, w_outer))[0].astype(jnp.bfloat16)
    grad_w_inner = weight_grad(middle_low, grad_inner)
    grad_b_inner = column_sum(grad_inner)
    grad_middle = grad_second + back_product(grad_inner, w_inner)
    grad_gain_first = jnp.sum(grad_middle * normed_first, 0)
    grad_bias_first = jnp.sum(grad_middle, 0)
    grad_first = norm_back(grad_middle, normed_first, inverse_first, gain_first)
    grad_branch = grad_first.astype(jnp.bfloat16)
    grad_w_out = weight_grad(context_low, grad_branch)
    grad_b_out = column_sum(grad_branch)
    grad_context = (
        back_product(grad_branch, w_out).astype(jnp.bfloat16).reshape(rows, stretch, heads, depth)
    )
    delta = jnp.einsum("rqhd,rhqd->rhq", grad_context.astype(jnp.float32), context)
    pieces = (
        lax.all_gather(keys_own, "blk", axis=1, tiled=True),
        lax.all_gather(values_own, "blk", axis=1, tiled=True),
    )
    keys_piece = pieces[0].reshape(rows, -1, heads, depth)
    values_piece = pieces[1].reshape(rows, -1, heads, depth)
    probs, grad_scores = score_grads(
        query_heads, keys_piece, values_piece, grad_context, log_total, delta, score_scale
    )
    grad_query = score_scale * jnp.einsum(
        "rhqk,rkhd->rqhd", grad_scores, keys_piece, preferred_element_type=jnp.float32
    )
    log_all, delta_all = (
        lax.all_gather(
            log_total.transpose(0, 2, 1).astype(jnp.bfloat16), "blk", axis=1, tiled=True
        ).astype(jnp.float32),
        lax.all_gather(
            delta.transpose(0, 2, 1).astype(jnp.bfloat16), "blk", axis=1, tiled=True
        ).astype(jnp.float32),
    )
    key_heads = keys_own.reshape(rows, stretch, heads, depth)
    value_heads = values_own.reshape(rows, stretch, heads, depth)
    pieces = (
        lax.all_gather(queries.reshape(rows, stretch, width), "blk", axis=1, tiled=True),
        lax.all_gather(grad_context.reshape(rows, stretch, width), "blk", axis=1, tiled=True),
    )
    query_piece = pieces[0].reshape(rows, -1, heads, depth)
    context_piece = pieces[1].reshape(rows, -1, heads, depth)
    log_piece = log_all.transpose(0, 2, 1)
    delta_piece = delta_all.transpose(0, 2, 1)
    probs, grad_scores = score_grads(
        query_piece, key_heads, value_heads, context_piece, log_piece, delta_piece, score_scale
    )
    grad_key_sum = score_scale * jnp.einsum(
        "rhqk,rqhd->rkhd", grad_scores, query_piece, preferred_element_type=jnp.float32
    )
    grad_value_sum = jnp.einsum(
        "rhqk,rqhd->rkhd",
        probs.astype(jnp.bfloat16),
        context_piece,
        preferred_element_type=jnp.float32,
    )
    grad_key_sum, grad_value_sum = (grad_key_sum, grad_value_sum)
    grad_keys = grad_key_sum.reshape(rows * stretch, width).astype(jnp.bfloat16)
    grad_values = grad_value_sum.reshape(rows * stretch, width).astype(jnp.bfloat16)
    grad_queries = grad_query.reshape(rows * stretch, width).astype(jnp.bfloat16)
    grad_w_query = weight_grad(flat, grad_queries)
    grad_b_query = column_sum(grad_queries)
    grad_w_key = weight_grad(flat, grad_keys)
    grad_w_value = weight_grad(flat, grad_values)
    grad_b_value = column_sum(grad_values)
    grad_input = (
        grad_first
        + back_product(grad_queries, w_query)
        + back_product(grad_keys, w_key)
        + back_product(grad_values, w_value)
    )
    grad_tokens = grad_input.astype(jnp.bfloat16).reshape(rows, stretch, width)
    shares = (
        lax.psum_scatter(
            grad_w_query.astype(jnp.bfloat16), "batch", scatter_dimension=0, tiled=True
        ).astype(jnp.float32),
        lax.psum_scatter(
            grad_b_query.astype(jnp.bfloat16), "batch", scatter_dimension=0, tiled=True
        ).astype(jnp.float32),
        lax.psum_scatter(
            grad_w_key.astype(jnp.bfloat16), "batch", scatter_dimension=0, tiled=True
        ).astype(jnp.float32),
        lax.psum_scatter(
            grad_w_value.astype(jnp.bfloat16), "batch", scatter_dimension=0, tiled=True
        ).astype(jnp.float32),
        lax.psum_scatter(
            grad_b_value.astype(jnp.bfloat16), "batch", scatter_dimension=0, tiled=True
        ).astype(jnp.float32),
        lax.psum_scatter(
            grad_w_out.astype(jnp.bfloat16), "batch", scatter_dimension=0, tiled=True
        ).astype(jnp.float32),
        lax.psum_scatter(
            grad_b_out.astype(jnp.bfloat16), "batch", scatter_dimension=0, tiled=True
        ).astype(jnp.float32),
        lax.psum_scatter(
            grad_gain_first.astype(jnp.bfloat16), "batch", scatter_dimension=0, tiled=True
        ).astype(jnp.float32),
        lax.psum_scatter(
            grad_bias_first.astype(jnp.bfloat16), "batch", scatter_dimension=0, tiled=True
        ).astype(jnp.float32),
        lax.psum_scatter(
            grad_w_inner.astype(jnp.bfloat16), "batch", scatter_dimension=0, tiled=True
        ).astype(jnp.float32),
        lax.psum_scatter(
            grad_b_inner.astype(jnp.bfloat16), "batch", scatter_dimension=0, tiled=True
        ).astype(jnp.float32),
        lax.psum_scatter(
            grad_w_outer.astype(jnp.bfloat16), "batch", scatter_dimension=0, tiled=True
        ).astype(jnp.float32),
        lax.psum_scatter(
            grad_b_outer.astype(jnp.bfloat16), "batch", scatter_dimension=0, tiled=True
        ).astype(jnp.float32),
        lax.psum_scatter(
            grad_gain_second.astype(jnp.bfloat16), "batch", scatter_dimension=0, tiled=True
        ).astype(jnp.float32),
        lax.psum_scatter(
            grad_bias_second.astype(jnp.bfloat16), "batch", scatter_dimension=0, tiled=True
        ).astype(jnp.float32),
    )
    totals = (
        lax.psum(shares[0].astype(jnp.bfloat16), "blk").astype(jnp.float32),
        lax.psum(shares[1].astype(jnp.bfloat16), "blk").astype(jnp.float32),
        lax.psum(shares[2].astype(jnp.bfloat16), "blk").astype(jnp.float32),
        lax.psum(shares[3].astype(jnp.bfloat16), "blk").astype(jnp.float32),
        lax.psum(shares[4].astype(jnp.bfloat16), "blk").astype(jnp.float32),
        lax.psum(shares[5].astype(jnp.bfloat16), "blk").astype(jnp.float32),
        lax.psum(shares[6].astype(jnp.bfloat16), "blk").astype(jnp.float32),
        lax.psum(shares[7].astype(jnp.bfloat16), "blk").astype(jnp.float32),
        lax.psum(shares[8].astype(jnp.bfloat16), "blk").astype(jnp.float32),
        lax.psum(shares[9].astype(jnp.bfloat16), "blk").astype(jnp.float32),
        lax.psum(shares[10].astype(jnp.bfloat16), "blk").astype(jnp.float32),
        lax.psum(shares[11].astype(jnp.bfloat16), "blk").astype(jnp.float32),
        lax.psum(shares[12].astype(jnp.bfloat16), "blk").astype(jnp.float32),
        lax.psum(shares[13].astype(jnp.bfloat16), "blk").astype(jnp.float32),
        lax.psum(shares[14].astype(jnp.bfloat16), "blk").astype(jnp.float32),
    )
    return (output, grad_tokens) + tuple(totals)


def solution(mesh):
    placed = (
        P("batch", "blk", None),
        P("batch", "blk"),
        P("batch", "blk", None),
        P("batch", None),
        P("batch"),
        P("batch", None),
        P("batch", None),
        P("batch"),
        P("batch", None),
        P("batch"),
        P("batch"),
        P("batch"),
        P("batch", None),
        P("batch"),
        P("batch", None),
        P("batch"),
        P("batch"),
        P("batch"),
    )
    return jax.shard_map(
        body,
        mesh=mesh,
        in_specs=placed,
        out_specs=(
            P("batch", "blk", None),
            P("batch", "blk", None),
            P("batch", None),
            P("batch"),
            P("batch", None),
            P("batch", None),
            P("batch"),
            P("batch", None),
            P("batch"),
            P("batch"),
            P("batch"),
            P("batch", None),
            P("batch"),
            P("batch", None),
            P("batch"),
            P("batch"),
            P("batch"),
        ),
        check_vma=False,
    )
```

profile of v0, /device:TPU:0, one launch (start us, length us, event | category | flops | bytes accessed | tf_op | source)
XLA Modules:
  0.0 1219.2 jit_solution(6976624331677419129)
XLA Ops:
  9.5 41.9 %all-gather.13.cloned.1.call-done = bf16[768,768]{1,0:T(8,128)(2,1)} async-done(((bf16[48,768]{1,0:T(8,128)(2,1)}), bf16[768,768]{1,0:T(8,128)(2,1)}) %all-gather.13.cloned.1.call-update) | async-done | bytes 1179664 | tf_op jit(solution)/shard_map/all_gather | solution.py:97
  51.4 6.6 convolution_convert_fusion.3
  61.9 60.0 %all-reduce.19 = (bf16[768]{0:T(1024)(128)(2,1)S(1)}, bf16[768]{0:T(1024)(128)(2,1)S(1)}, bf16[768]{0:T(1024)(128)(2,1)S(1)}, bf16[768]{0:T(1024)(128)(2,1)S(1)}...) all-reduce(bf16[768]{0:T(1024)(128)(2,1)S(1)} %dynamic-update-slice, ...), channel_id=1, replica_groups=mesh['batch'=16,'blk'=2] {'batch'}, use_global_device_ids=true, to_apply=%add | all-reduce | flops 8448 | bytes 33792
  121.9 6.5 add_convert_fusion.3
  130.8 6.5 add_convert_fusion.4
  143.2 5.4 copy.61
  151.5 4.9 copy.73
  163.1 49.1 %all-gather.15.cloned.1.call-done = bf16[8,512,768]{2,1,0:T(8,128)(2,1)} async-done(((bf16[8,256,768]{2,1,0:T(8,128)(2,1)}), bf16[8,512,768]{2,1,0:T(8,128)(2,1)}) %all-gather.15.cloned.1.call-update) | async-done | bytes 6291472 | tf_op jit(solution)/shard_map/all_gather | solution.py:127
  212.2 8.8 copy.62
  221.0 22.1 %multiply_reduce_fusion = (f32[8,12,256]{2,1,0:T(8,128)S(1)}, f32[8,12,256,512]{3,2,1,0:T(8,128)}) fusion(bf16[8,512,12,64]{1,3,2,0:T(8,128)(2,1)} %bitcast.150, bf16[8,256,12,64]{1,0,3,2:T(8,128)(2,1)} %bitcast.157), kind=kOutput, calls=%fused_computation.7 | convolution fusion | flops 1635753984 | bytes 59867136 | tf_op jit(solution)/shard_map/rqhd,rkhd->rhqk/dot_general | solution.py:134
  243.1 21.2 %fusion = f32[8,12,256]{2,1,0:T(8,128)S(1)} fusion(f32[8,12,256,512]{3,2,1,0:T(8,128)} %get-tuple-element.120, f32[8,12,256]{2,1,0:T(8,128)S(1)} %broadcast_maximum_fusion), kind=kLoop, calls=%fused_computation.4 | loop fusion | flops 37724160 | bytes 50528256 | tf_op jit(solution)/shard_map/reduce_sum | solution.py:139
  265.0 29.0 %all-gather.19.cloned.1.call-done = bf16[8,512,768]{2,1,0:T(8,128)(2,1)} async-done(((bf16[8,256,768]{2,1,0:T(8,128)(2,1)}), bf16[8,512,768]{2,1,0:T(8,128)(2,1)}) %all-gather.19.cloned.1.call-update) | async-done | bytes 6291472 | tf_op jit(solution)/shard_map/all_gather | solution.py:128
  294.0 8.7 copy.64
  302.8 23.9 %fusion.23 = (bf16[8,256,12,64]{1,3,2,0:T(8,128)(2,1)}, f32[8,12,256,64]{2,3,1,0:T(8,128)}) fusion(f32[8,256,12]{1,2,0:T(8,128)S(1)} %bitcast.185, bf16[8,512,12,64]{1,3,2,0:T(8,128)(2,1)} %bitcast.174, f32[8,12,256,512]{3,2,1,0:T(8,128)} %get-tuple-element.120, f32[8,12,256]{2,1,0:T(8,128)S(1)} %broadcast_maximum_fusion), kind=kOutput, calls=%fused_computation.37 | convolution fusion | flops 1651507200 | bytes 66256896 | tf_op jit(solution)/shard_map/rhqk,rkhd->rhqd/dot_general | solution.py:140
  334.6 6.4 fusion.61
  345.0 6.4 all_gather.83
  352.1 65.3 %all-gather.27.cloned.1.call-done = bf16[8,512,768]{2,1,0:T(8,128)(2,1)} async-done(((bf16[8,256,768]{2,1,0:T(8,128)(2,1)}), bf16[8,512,768]{2,1,0:T(8,128)(2,1)}) %all-gather.27.cloned.1.call-update) | async-done | bytes 6291472 | tf_op jit(solution)/shard_map/all_gather | solution.py:215
  417.4 8.9 copy.69
  426.3 21.1 %fusion.31 = f32[8,12,512,256]{3,2,1,0:T(8,128)} fusion(bf16[8,512,12,64]{1,3,2,0:T(8,128)(2,1)} %bitcast.152, bf16[8,256,12,64]{1,0,3,2:T(8,128)(2,1)S(1)} %bitcast.156), kind=kOutput, calls=%fused_computation.73 | convolution fusion | flops 1610612736 | bytes 59768832 | tf_op jit(solution)/shard_map/rqhd,rkhd->rhqk/dot_general | solution.py:47
  447.4 24.4 %all-gather.23.cloned.1.call-done = bf16[768,3072]{1,0:T(8,128)(2,1)} async-done(((bf16[48,3072]{1,0:T(8,128)(2,1)}), bf16[768,3072]{1,0:T(8,128)(2,1)}) %all-gather.23.cloned.1.call-update) | async-done | bytes 4718608 | tf_op jit(solution)/shard_map/all_gather | solution.py:104
  471.8 70.3 %multiply_convert_fusion.2 = (bf16[2048,3072]{1,0:T(8,128)(2,1)}, f32[2048,3072]{1,0:T(8,128)}, f32[2048,3072]{1,0:T(8,128)}) fusion(f32[3072]{0:T(1024)S(1)} %convert_element_type.289, bf16[768,3072]{1,0:T(8,128)(2,1)} %all-gather.23.cloned.1.call-done, f32[2048,768]{1,0:T(8,128)} %copy-done.3, f32[768]{0:T(1024)S(1)} %convert_element_type.287, ...), kind=kOutput, calls=%fused_computation.15 | convolution fusion | flops 10086776832 | bytes 73959424 | tf_op jit(solution)/shard_map/dot_general | solution.py:157
  542.1 16.2 %fusion.62 = (f32[2048]{0:T(1024)S(1)}, f32[2048,768]{1,0:T(8,128)S(1)}) fusion(f32[768]{0:T(1024)S(1)} %copy-done.38, bf16[2048,3072]{1,0:T(8,128)(2,1)} %get-tuple-element.113, bf16[3072,768]{1,0:T(8,128)(2,1)} %all-gather.25.cloned.1.call-done, f32[768]{0:T(1024)S(1)} %convert_element_type.287, f32[768]{0:T(1024)S(1)} %convert_element_type.286, ...), kind=kOutput, calls=%fused_computation.116 | convolution fusion | flops 9674684416 | bytes 29918208 | tf_op jit(solution)/shard_map/dot_general | solution.py:164
  565.8 4.9 convert_reduce_fusion.1
  570.7 29.1 %fusion.67 = (bf16[3072]{0:T(1024)(128)(2,1)}, bf16[2048,3072]{1,0:T(8,128)(2,1)}) fusion(f32[2048,3072]{1,0:T(8,128)} %get-tuple-element.114, bf16[3072,768]{1,0:T(8,128)(2,1)S(1)} %bitcast.190, f32[2048,768]{1,0:T(8,128)} %get-tuple-element.110, f32[2048,3072]{1,0:T(8,128)} %get-tuple-element.125, f32[3072]{0:T(1024)S(1)} %convert_element_type.289), kind=kOutput, calls=%fused_computation.119 | convolution fusion | flops 9765909504 | bytes 73943040 | tf_op jit(solution)/shard_map/dot_general | solution.py:36
  599.8 19.4 %multiply_reduce_fusion.3 = (bf16[768]{0:T(1024)(128)(2,1)}, f32[2048]{0:T(1024)S(1)}, f32[2048]{0:T(1024)S(1)}, bf16[768]{0:T(1024)(128)(2,1)}, f32[2048,768]{1,0:T(8,128)S(1)}) fusion(f32[2048,768]{1,0:T(8,128)} %copy-done.3, f32[2048]{0:T(1024)S(1)} %add_rsqrt_fusion.1, f32[2048]{0:T(1024)S(1)} %broadcast_multiply_fusion.4, ...), kind=kOutput, calls=%fused_computation.40 | convolution fusion | flops 9679398912 | bytes 36214784 | tf_op jit(solution)/shard_map/dot_general | solution.py:36
  619.2 5.3 convert_reduce_fusion
  633.3 4.6 copy.95
  640.5 6.6 multiply_reduce_fusion.1
  647.1 29.8 %fusion.63 = (bf16[12,64]{1,0:T(8,128)(2,1)}, bf16[8,256,12,64]{1,3,2,0:T(8,128)(2,1)}) fusion(bf16[8,512,12,64]{1,3,2,0:T(8,128)(2,1)} %bitcast.151, f32[8,12,256,512]{3,2,1,0:T(8,128)} %get-tuple-element.120, f32[8,12,256]{2,1,0:T(8,128)S(1)} %multiply_reduce_fusion.1, f32[8,12,256]{2,1,0:T(8,128)S(1)} %copy-done.19, ...), kind=kOutput, calls=%fused_computation.117 | convolution fusion | flops 3288857856 | bytes 69404160 | tf_op jit(solution)/shard_map/rhqk,rkhd->rqhd/dot_general | solution.py:201
  687.8 6.8 all_gather.85
  695.4 22.9 %all-gather.29.cloned.1.call-done = bf16[8,512,768]{2,1,0:T(8,128)(2,1)} async-done(((bf16[8,256,768]{2,1,0:T(8,128)(2,1)}), bf16[8,512,768]{2,1,0:T(8,128)(2,1)}) %all-gather.29.cloned.1.call-update) | async-done | bytes 6291472 | tf_op jit(solution)/shard_map/all_gather | solution.py:216
  718.4 9.1 copy.72
  727.4 27.0 %fusion.28 = bf16[8,256,12,64]{1,3,2,0:T(8,128)(2,1)} fusion(bf16[8,512,12,64]{1,3,2,0:T(8,128)(2,1)} %bitcast.153, f32[8,12,512,256]{3,2,1,0:T(8,128)} %fusion.31, f32[8,12,512]{2,1,0:T(8,128)} %convert_bitcast_fusion.1, f32[8,12,512]{2,1,0:T(8,128)S(1)} %copy-done.16, bf16[8,512,12,64]{1,3,2,0:T(8,128)(2,1)} %bitcast.154, ...), kind=kOutput, calls=%fused_computation.70 | convolution fusion | flops 3287285760 | bytes 69599232 | tf_op jit(solution)/shard_map/rhqk,rqhd->rkhd/dot_general | solution.py:225
  754.5 4.1 copy.75
  765.5 20.1 %fusion.66 = (bf16[12,64]{1,0:T(8,128)(2,1)S(1)}, bf16[8,256,12,64]{1,3,2,0:T(8,128)(2,1)S(1)}) fusion(bf16[8,512,12,64]{1,3,2,0:T(8,128)(2,1)} %bitcast.155, f32[8,12,512,256]{3,2,1,0:T(8,128)} %fusion.31, f32[8,12,512]{2,1,0:T(8,128)S(1)} %copy-done.16), kind=kOutput, calls=%fused_computation.118 | convolution fusion | flops 1651506432 | bytes 59966976 | tf_op jit(solution)/shard_map/rhqk,rqhd->rkhd/dot_general | solution.py:228
  795.0 7.5 convolution_convert_fusion.4
  802.6 18.0 %convolution_convert_fusion.1 = bf16[768,3072]{1,0:T(8,128)(2,1)} fusion(bf16[2048,3072]{1,0:T(8,128)(2,1)} %get-tuple-element.134, f32[2048,768]{1,0:T(8,128)} %copy-done.3, f32[768]{0:T(1024)S(1)} %copy-done.36, f32[768]{0:T(1024)S(1)} %copy-done.28, f32[2048]{0:T(1024)S(1)} %add_rsqrt_fusion.1, f32[2048]{0:T(1024)S(1)} %broadcast_multiply_fusion.4), kind=kOutput, calls=%fused_computation.65 | convolution fusion | flops 9673900032 | bytes 23615488 | tf_op jit(solution)/shard_map/dot_general | solution.py:30
  820.7 16.4 %convolution_convert_fusion = bf16[3072,768]{1,0:T(8,128)(2,1)} fusion(bf16[2048,3072]{1,0:T(8,128)(2,1)} %get-tuple-element.113, f32[2048,768]{1,0:T(8,128)} %get-tuple-element.110), kind=kOutput, calls=%fused_computation.64 | convolution fusion | flops 9667608576 | bytes 23592960 | tf_op jit(solution)/shard_map/dot_general | solution.py:30
  839.1 7.5 fusion.68
  848.4 7.5 fusion.69
  857.6 43.9 %reduce-scatter.23.cloned.1.call-done = bf16[48,768]{1,0:T(8,128)(2,1)} async-done(((bf16[768,768]{1,0:T(8,128)(2,1)}), bf16[48,768]{1,0:T(8,128)(2,1)}) %reduce-scatter.23.cloned.1.call-update) | async-done | bytes 73744
  903.2 58.9 %reduce-scatter.13.cloned.1.call-done = bf16[48,768]{1,0:T(8,128)(2,1)} async-done(((bf16[768,768]{1,0:T(8,128)(2,1)}), bf16[48,768]{1,0:T(8,128)(2,1)}) %reduce-scatter.13.cloned.1.call-update) | async-done | bytes 73744 | tf_op jit(solution)/shard_map/reduce_scatter | solution.py:266
  962.2 78.3 %reduce-scatter.15.cloned.1.call-done = bf16[48,3072]{1,0:T(8,128)(2,1)} async-done(((bf16[768,3072]{1,0:T(8,128)(2,1)}), bf16[48,3072]{1,0:T(8,128)(2,1)}) %reduce-scatter.15.cloned.1.call-update) | async-done | bytes 294928 | tf_op jit(solution)/shard_map/reduce_scatter | solution.py:278
  1040.5 78.8 %reduce-scatter.17.cloned.1.call-done = bf16[192,768]{1,0:T(8,128)(2,1)} async-done(((bf16[3072,768]{1,0:T(8,128)(2,1)}), bf16[192,768]{1,0:T(8,128)(2,1)}) %reduce-scatter.17.cloned.1.call-update) | async-done | bytes 294928 | tf_op jit(solution)/shard_map/reduce_scatter | solution.py:284
  1119.4 9.4 add_convert_fusion.1
  1129.0 58.1 %all-reduce.18 = (bf16[768]{0:T(1024)(128)(2,1)S(1)}, bf16[768]{0:T(1024)(128)(2,1)S(1)}, bf16[768]{0:T(1024)(128)(2,1)S(1)}, bf16[768]{0:T(1024)(128)(2,1)S(1)}...) all-reduce(bf16[768]{0:T(1024)(128)(2,1)S(1)} %dynamic-update-slice, ...), channel_id=1, replica_groups=mesh['batch'=16,'blk'=2] {'batch'}, use_global_device_ids=true, to_apply=%add.8 | all-reduce | flops 9984 | bytes 39936
  1187.7 5.0 all-reduce.20
  1197.4 4.5 add_convert_fusion.2
  (253 shorter events, 104.1 us)
Async XLA Ops:
  7.2 44.2 %all-gather.13.cloned.1.call-start = ((), (), s32[]{:S(2)}) async-start(), calls=%async_computation.7 | async-start | bytes 1253376 | tf_op jit(solution)/shard_map/all_gather | solution.py:97
  7.9 114.0 %all-gather.17.cloned.1.call-start = ((), (), s32[]{:S(2)}) async-start(), calls=%async_computation.9 | async-start | bytes 1253376 | tf_op jit(solution)/shard_map/all_gather | solution.py:98
  8.7 122.1 %all-gather.11.cloned.1.call-start = ((), (), s32[]{:S(2)}) async-start(), calls=%async_computation.6 | async-start | bytes 1253376 | tf_op jit(solution)/shard_map/all_gather | solution.py:95
  9.4 202.8 %all-gather.15.cloned.1.call-start = ((), (), s32[]{:S(2)}) async-start(), calls=%async_computation.8 | async-start | bytes 9437184 | tf_op jit(solution)/shard_map/all_gather | solution.py:127
  51.4 8.6 copy-start.46
  51.4 8.9 copy-start.47
  51.4 9.1 copy-start.48
  51.4 9.3 copy-start.49
  51.4 9.6 copy-start.50
  51.4 9.8 copy-start.51
  51.4 10.0 copy-start.52
  51.4 10.3 copy-start.53
  58.0 236.0 %all-gather.19.cloned.1.call-start = ((), (), s32[]{:S(2)}) async-start(), calls=%async_computation.10 | async-start | bytes 9437184 | tf_op jit(solution)/shard_map/all_gather | solution.py:128
  128.4 206.1 %all-gather.21.cloned.1.call-start = ((), (), s32[]{:S(2)}) async-start(), calls=%async_computation.11 | async-start | bytes 1253376 | tf_op jit(solution)/shard_map/all_gather | solution.py:100
  129.0 288.4 %all-gather.27.cloned.1.call-start = ((), (), s32[]{:S(2)}) async-start(), calls=%async_computation.14 | async-start | bytes 9437184 | tf_op jit(solution)/shard_map/all_gather | solution.py:215
  129.1 10.5 copy-start.32
  129.1 11.1 copy-start.1
  137.3 334.5 %all-gather.23.cloned.1.call-start = ((), (), s32[]{:S(2)}) async-start(), calls=%async_computation.12 | async-start | bytes 5013504 | tf_op jit(solution)/shard_map/all_gather | solution.py:104
  138.1 404.0 %all-gather.25.cloned.1.call-start = ((), (), s32[]{:S(2)}) async-start(), calls=%async_computation.13 | async-start | bytes 5013504 | tf_op jit(solution)/shard_map/all_gather | solution.py:106
  138.8 579.5 %all-gather.29.cloned.1.call-start = ((), (), s32[]{:S(2)}) async-start(), calls=%async_computation.15 | async-start | bytes 9437184 | tf_op jit(solution)/shard_map/all_gather | solution.py:216
  138.9 480.3 %copy-start.27 = (f32[768]{0:T(1024)}, f32[768]{0:T(1024)S(1)}, u32[]{:S(2)}) copy-start(f32[768]{0:T(1024)S(1)} %convert_element_type.286) | copy-start | bytes 9220
  138.9 403.2 %copy-start.35 = (f32[768]{0:T(1024)}, f32[768]{0:T(1024)S(1)}, u32[]{:S(2)}) copy-start(f32[768]{0:T(1024)S(1)} %convert_element_type.287) | copy-start | bytes 9220
  264.3 38.4 %copy-start.14 = (f32[8,12,256]{2,1,0:T(8,128)}, f32[8,12,256]{2,1,0:T(8,128)S(1)}, u32[]{:S(2)}) copy-start(f32[8,12,256]{2,1,0:T(8,128)S(1)} %fusion) | copy-start | bytes 294916
  471.8 70.3 %copy-start.38 = (f32[768]{0:T(1024)S(1)}, f32[768]{0:T(1024)}, u32[]{:S(2)}) copy-start(f32[768]{0:T(1024)} %convert_element_type.291) | copy-start | bytes 9220
  559.3 11.4 copy-start.20
  562.6 8.1 slice-start
  630.0 7.9 copy-start.6
  637.9 208.8 %reduce-scatter.19.cloned.1.call-start = ((), (), s32[]{:S(2)}) async-start(), calls=%async_computation.19 | async-start | bytes 1253376
  695.4 32.1 %copy-start.11 = (bf16[96,8,8,256]{3,2,1,0:T(8,128)(2,1)S(1)}, bf16[96,8,8,256]{3,2,1,0:T(8,128)(2,1)}, u32[]{:S(2)}) copy-start(bf16[96,8,8,256]{3,2,1,0:T(8,128)(2,1)} %copy.98) | copy-start | bytes 9437188
  695.4 32.1 %copy-start.16 = (f32[8,12,512]{2,1,0:T(8,128)S(1)}, f32[8,12,512]{2,1,0:T(8,128)}, u32[]{:S(2)}) copy-start(f32[8,12,512]{2,1,0:T(8,128)} %convert_bitcast_fusion.2) | copy-start | bytes 589828
  695.4 160.5 %reduce-scatter.21.cloned.1.call-start = ((), (), s32[]{:S(2)}) async-start(), calls=%async_computation.20 | async-start | bytes 1253376
  765.4 136.1 %reduce-scatter.23.cloned.1.call-start = ((), (), s32[]{:S(2)}) async-start(), calls=%async_computation.21 | async-start | bytes 1253376
  794.9 167.2 %reduce-scatter.13.cloned.1.call-start = ((), (), s32[]{:S(2)}) async-start(), calls=%async_computation.16 | async-start | bytes 1253376 | tf_op jit(solution)/shard_map/reduce_scatter | solution.py:266
  802.5 237.9 %reduce-scatter.15.cloned.1.call-start = ((), (), s32[]{:S(2)}) async-start(), calls=%async_computation.17 | async-start | bytes 5013504 | tf_op jit(solution)/shard_map/reduce_scatter | solution.py:278
  820.7 17.9 %copy-start.54 = (bf16[48]{0:T(256)(128)(2,1)S(1)}, bf16[48]{0:T(256)(128)(2,1)}, u32[]{:S(2)}) copy-start(bf16[48]{0:T(256)(128)(2,1)} %param.35) | copy-start | bytes 292
  820.7 18.4 %copy-start.37 = (bf16[12,64]{1,0:T(8,128)(2,1)S(1)}, bf16[12,64]{1,0:T(8,128)(2,1)}, u32[]{:S(2)}) copy-start(bf16[12,64]{1,0:T(8,128)(2,1)} %get-tuple-element.129) | copy-start | bytes 4612
  820.7 298.6 %reduce-scatter.17.cloned.1.call-start = ((), (), s32[]{:S(2)}) async-start(), calls=%async_computation.18 | async-start | bytes 5013504 | tf_op jit(solution)/shard_map/reduce_scatter | solution.py:284
  837.2 364.7 %all-reduce.24.cloned.1.call-start = ((), (), s32[]{:S(2)}) async-start(), calls=%async_computation.22 | async-start | bytes 2506752 | tf_op jit(solution)/shard_map/psum | solution.py:298
  1119.3 9.6 copy-start.29
  1119.3 9.6 copy-start.30
  1119.4 9.6 copy-start.31
  1119.4 9.6 copy-start.33
  1119.4 9.6 copy-start.34
  1119.4 9.6 copy-start.39
  1119.4 9.6 copy-start.40
  1119.4 78.0 %copy-start.18 = (f32[2048]{0:T(1024)S(1)}, f32[2048]{0:T(1024)}, u32[]{:S(2)}) copy-start(f32[2048]{0:T(1024)} %copy-done.17) | copy-start | bytes 24580
  1119.4 78.0 %copy-start.21 = (f32[2048]{0:T(1024)S(1)}, f32[2048]{0:T(1024)}, u32[]{:S(2)}) copy-start(f32[2048]{0:T(1024)} %copy-done.20) | copy-start | bytes 24580
  1119.4 78.0 %copy-start.24 = (f32[768]{0:T(1024)S(1)}, f32[768]{0:T(1024)}, u32[]{:S(2)}) copy-start(f32[768]{0:T(1024)} %copy-done.22) | copy-start | bytes 9220
  (26 other events, 131.1 us)
Sparse Core Ops, SparseCore 0:
  10.3 41.0 all-gather.12
  53.7 37.4 all-gather.16
  93.4 37.3 all-gather.10
  132.8 79.3 all-gather.14
  213.6 80.3 all-gather.18
  296.2 38.3 all-gather.20
  336.7 80.7 all-gather.26
  419.7 52.0 all-gather.22
  474.1 51.9 all-gather.24
  638.0 80.3 all-gather.28
  722.0 58.1 reduce-scatter.18
  783.7 57.0 reduce-scatter.20
  844.4 57.1 reduce-scatter.22
  905.0 57.1 reduce-scatter.12
  965.9 74.5 reduce-scatter.14
  1044.7 74.5 reduce-scatter.16
  1122.4 44.4 all-reduce.23
where the time goes:
time: 1230 us; the launch traced here: 1220 us
  waiting for transfers between devices  500 us (41%)
  matrix products  383 us (31%)
  blocking collectives  136 us (11%)
  local copies, waits for them, and re-layouts  116 us (9%)
  other arithmetic  65 us (5%)
  between operations  17.8 us (1%)
    unnamed x2, blocking collectives  118 us
    reduce_scatter x1, waiting for transfers between devices, body(): lax.psum_scatter(grad_w_outer.astype(jnp.bfloat16), 'batch', scatter_dime...  78.8 us
    reduce_scatter x1, waiting for transfers between devices, body(): lax.psum_scatter(grad_w_inner.astype(jnp.bfloat16), 'batch', scatter_dime...  78.3 us
    dot_general x6, matrix products, back_product(): lax.dot_general(grad, matrix, (((1,), (1,)), ((), ())), preferred_element...  75.9 us
    dot_general x1, matrix products, body(): jnp.dot(middle_low, w_inner, preferred_element_type=jnp.float32)  70.3 us
    all_gather x1, waiting for transfers between devices, body(): lax.all_gather(queries.reshape(rows, stretch, width), 'blk', axis=1, tile...  65.3 us
    reduce_scatter x1, waiting for transfers between devices, body(): lax.psum_scatter(grad_w_out.astype(jnp.bfloat16), 'batch', scatter_dimens...  58.9 us
    dot_general x6, matrix products, weight_grad(): lax.dot_general(left, right, (((0,), (0,)), ((), ())), preferred_element_...  50.8 us
  transfers between devices with their start and end apart: 17, of which 12 were waited for; matrix products, arithmetic and copies ran while one was open for 37% of the time, Pallas kernels for 0%

commit v1 on v0

v1 whole, which is shorter than its diff:
```python
import functools

import jax
import jax.numpy as jnp
from jax import lax
from jax.experimental import pallas as pl
from jax.experimental.pallas import tpu as pltpu
from jax.sharding import PartitionSpec as P

HEADS = 12
HEAD_DIM = 64
PAIR = 2 * HEAD_DIM
STAT_ROWS = 16
VMEM_BYTES = 60 * 2**20

epsilon = 1e-06
bf16 = jnp.bfloat16
f32 = jnp.float32

NN = (((1,), (0,)), ((), ()))
NT = (((1,), (1,)), ((), ()))
TN = (((0,), (0,)), ((), ()))

B_QUERY, B_VALUE, B_OUT, GAIN_1, BIAS_1, B_OUTER, GAIN_2, BIAS_2, B_INNER = range(9)


def mul(left, right, dims=NN):
    return lax.dot_general(left, right, dims, preferred_element_type=f32)


def row(ref, index):
    return ref[index : index + 1, :]


def halves(block):
    lane = lax.broadcasted_iota(jnp.int32, block.shape, 1)
    zero = jnp.zeros_like(block)
    return jnp.where(lane < HEAD_DIM, block, zero), jnp.where(lane < HEAD_DIM, zero, block)


def pair_at(p):
    return pl.ds(pl.multiple_of(p * PAIR, PAIR), PAIR)


def normalize(values):
    center = values - jnp.mean(values, -1, keepdims=True)
    inverse = lax.rsqrt(jnp.mean(center * center, -1, keepdims=True) + epsilon)
    return center * inverse, inverse


def norm_back(grad, normed, inverse, gain):
    scaled = grad * gain
    return inverse * (
        scaled
        - jnp.mean(scaled, -1, keepdims=True)
        - normed * jnp.mean(scaled * normed, -1, keepdims=True)
    )


def column_sum(values):
    return jnp.sum(values.astype(f32), 0, keepdims=True)


def project(x, w_ref, vec_ref, q_ref, k_ref, v_ref):
    width = x.shape[-1]
    q = (mul(x, w_ref[:, :width]) + row(vec_ref, B_QUERY)).astype(bf16)
    q_ref[...] = q * bf16(HEAD_DIM**-0.5)
    k_ref[...] = mul(x, w_ref[:, width : 2 * width]).astype(bf16)
    v_ref[...] = (mul(x, w_ref[:, 2 * width :]) + row(vec_ref, B_VALUE)).astype(bf16)


def attend(q_ref, k_ref, v_ref, c_ref, l_ref, stat):
    length = q_ref.shape[0]
    lane = lax.broadcasted_iota(jnp.int32, (length, 128), 1)

    def pair(p, carry):
        at = pair_at(p)
        q2, k2, v2 = q_ref[:, at], k_ref[:, at], v_ref[:, at]
        context = None
        for h, (k_one, v_one) in enumerate(zip(halves(k2), halves(v2))):
            scores = mul(q2, k_one, NT)
            best = jnp.max(scores, 1, keepdims=True)
            weights = jnp.exp(scores - best)
            total = jnp.sum(weights, 1, keepdims=True)
            part = mul(weights.astype(bf16), v_one) * (1.0 / total)
            context = part if context is None else context + part
            stat[...] = jnp.where(lane == 2 * p + h, best + jnp.log(total), stat[...])
        c_ref[:, at] = context.astype(bf16)
        return carry

    stat[...] = jnp.zeros_like(stat)
    lax.fori_loop(0, HEADS // 2, pair, 0, unroll=2)
    l_ref[...] = stat[...].T[:STAT_ROWS]


def attend_back(q_ref, k_ref, v_ref, g_ref, l_ref, d_ref, gq_ref, gk_ref, gv_ref, kt, gqt):
    kt[...] = (k_ref[...] * bf16(HEAD_DIM**-0.5)).T

    def pair(p, carry):
        at = pair_at(p)
        q2, g2 = q_ref[:, at], g_ref[:, at]
        ks, vs = halves(k_ref[:, at]), halves(v_ref[:, at])
        qs, gs = halves(q2), halves(g2)
        gk = gv = None
        for h in range(2):
            probs = jnp.exp(mul(ks[h], q2, NT) - l_ref[pl.ds(2 * p + h, 1), :])
            grad_probs = mul(vs[h], g2, NT)
            grad_scores = (probs * (grad_probs - d_ref[pl.ds(2 * p + h, 1), :])).astype(bf16)
            gk_one = mul(grad_scores, qs[h])
            gv_one = mul(probs.astype(bf16), gs[h])
            gk = gk_one if gk is None else gk + gk_one
            gv = gv_one if gv is None else gv + gv_one
            rows = pl.ds(pl.multiple_of((2 * p + h) * HEAD_DIM, HEAD_DIM), HEAD_DIM)
            gqt[rows, :] = mul(kt[rows, :], grad_scores).astype(bf16)
        gk_ref[:, at] = gk.astype(bf16)
        gv_ref[:, at] = gv.astype(bf16)
        return carry

    lax.fori_loop(0, HEADS // 2, pair, 0, unroll=2)
    gq_ref[...] = gqt[...].T


def feed_forward(
    x, cb, cot, wo_ref, wi_ref, wu_ref, vec_ref, out_ref, mid_ref, gf_ref, ga_ref, gc_ref, d_ref, h_ref, gu_ref, sums_ref
):
    width = x.shape[-1]
    chunks = wi_ref.shape[1] // width
    gain_1, gain_2 = row(vec_ref, GAIN_1), row(vec_ref, GAIN_2)
    normed_1, inverse_1 = normalize(x.astype(f32) + (mul(cb, wo_ref[...]) + row(vec_ref, B_OUT)))
    middle = normed_1 * gain_1 + row(vec_ref, BIAS_1)
    mid = middle.astype(bf16)
    mid_ref[...] = mid
    total = middle + row(vec_ref, B_OUTER)
    for c in range(chunks):
        at = slice(c * width, (c + 1) * width)
        inner = mul(mid, wi_ref[:, at]) + row(vec_ref, B_INNER + c)
        cdf = 0.5 + 0.5 * lax.erf(inner * (0.5**0.5))
        hidden = (inner * cdf).astype(bf16)
        h_ref[:, at] = hidden
        slope = cdf + inner * (jnp.exp(inner * inner * -0.5) * ((0.5 / jnp.pi) ** 0.5))
        gu_ref[:, at] = slope.astype(bf16)
        total = total + mul(hidden, wu_ref[at, :])
    normed_2, inverse_2 = normalize(total)
    out_ref[...] = (normed_2 * gain_2 + row(vec_ref, BIAS_2)).astype(bf16)
    grad = cot.astype(f32)
    sums_ref[GAIN_2 : GAIN_2 + 1, :] += column_sum(grad * normed_2)
    sums_ref[BIAS_2 : BIAS_2 + 1, :] += column_sum(grad)
    grad_2 = norm_back(grad, normed_2, inverse_2, gain_2)
    gf = grad_2.astype(bf16)
    gf_ref[...] = gf
    sums_ref[B_OUTER : B_OUTER + 1, :] += column_sum(gf)
    grad_mid = grad_2
    for c in range(chunks):
        at = slice(c * width, (c + 1) * width)
        gu = (mul(gf, wu_ref[at, :], NT) * gu_ref[:, at].astype(f32)).astype(bf16)
        gu_ref[:, at] = gu
        sums_ref[B_INNER + c : B_INNER + c + 1, :] += column_sum(gu)
        grad_mid = grad_mid + mul(gu, wi_ref[:, at], NT)
    sums_ref[GAIN_1 : GAIN_1 + 1, :] += column_sum(grad_mid * normed_1)
    sums_ref[BIAS_1 : BIAS_1 + 1, :] += column_sum(grad_mid)
    ga = norm_back(grad_mid, normed_1, inverse_1, gain_1).astype(bf16)
    ga_ref[...] = ga
    sums_ref[B_OUT : B_OUT + 1, :] += column_sum(ga)
    gc = mul(ga, wo_ref[...], NT).astype(bf16)
    gc_ref[...] = gc
    product = gc.astype(f32) * cb.astype(f32)
    high = product.astype(bf16)
    low = (product - high.astype(f32)).astype(bf16)
    head = lax.broadcasted_iota(jnp.int32, (STAT_ROWS, width), 0)
    column = lax.broadcasted_iota(jnp.int32, (STAT_ROWS, width), 1)
    pick = jnp.where(column // HEAD_DIM == head, 1.0, 0.0).astype(bf16)
    d_ref[...] = mul(pick, high, NT) + mul(pick, low, NT)


def spec(shape, pipelined=True):
    zeros = (0,) * (len(shape) - 1)
    if pipelined:
        return pl.BlockSpec(shape, lambda i: (i,) + zeros)
    return pl.BlockSpec(shape, lambda i: (0,) + zeros)


def whole_vmem():
    return pl.BlockSpec(memory_space=pltpu.VMEM)


def params():
    return pltpu.CompilerParams(vmem_limit_bytes=VMEM_BYTES, dimension_semantics=("arbitrary",))


def attention_call(x, w_qkv, vec):
    count, length, width = x.shape
    block = (None, length, width)

    def kernel(x_ref, w_ref, vec_ref, q_ref, k_ref, v_ref, c_ref, l_ref, stat):
        project(x_ref[...], w_ref, vec_ref, q_ref, k_ref, v_ref)
        attend(q_ref, k_ref, v_ref, c_ref, l_ref, stat)

    seq = jax.ShapeDtypeStruct(x.shape, bf16)
    return pl.pallas_call(
        kernel,
        grid=(count,),
        in_specs=[spec(block), whole_vmem(), whole_vmem()],
        out_specs=[spec(block)] * 4 + [spec((None, STAT_ROWS, length))],
        out_shape=[seq] * 4 + [jax.ShapeDtypeStruct((count, STAT_ROWS, length), f32)],
        scratch_shapes=[pltpu.VMEM((length, 128), f32)],
        compiler_params=params(),
        name="attention",
    )(x, w_qkv, vec)


def feed_forward_call(x, cb, cot, w_out, w_inner, w_outer, vec):
    count, length, width = x.shape
    inner = w_inner.shape[1]
    block, wide = (None, length, width), (None, length, inner)

    def kernel(x_ref, cb_ref, cot_ref, wo, wi, wu, vec_ref, out, mid, gf, ga, gc, d, h, gu, sums):
        @pl.when(pl.program_id(0) == 0)
        def _():
            sums[...] = jnp.zeros_like(sums)

        feed_forward(
            x_ref[...], cb_ref[...], cot_ref[...], wo, wi, wu, vec_ref, out, mid, gf, ga, gc, d, h, gu, sums
        )

    seq = jax.ShapeDtypeStruct(x.shape, bf16)
    seq_wide = jax.ShapeDtypeStruct((count, length, inner), bf16)
    return pl.pallas_call(
        kernel,
        grid=(count,),
        in_specs=[spec(block)] * 3 + [whole_vmem()] * 4,
        out_specs=[spec(block)] * 5
        + [spec((None, STAT_ROWS, length)), spec(wide), spec(wide), spec((16, width), False)],
        out_shape=[seq] * 5
        + [
            jax.ShapeDtypeStruct((count, STAT_ROWS, length), f32),
            seq_wide,
            seq_wide,
            jax.ShapeDtypeStruct((16, width), f32),
        ],
        compiler_params=params(),
        name="feed_forward",
    )(x, cb, cot, w_out, w_inner, w_outer, vec)


def weight_grad_call(left, right, over_left):
    tokens, rows = left.shape
    columns = right.shape[1]
    step = min(rows, columns)

    def kernel(left_ref, right_ref, out_ref):
        out_ref[...] = mul(left_ref[...], right_ref[...], TN).astype(bf16)

    if over_left:
        grid, left_map, right_map, out_map = rows // step, lambda i: (0, i), lambda i: (0, 0), lambda i: (i, 0)
    else:
        grid, left_map, right_map, out_map = columns // step, lambda i: (0, 0), lambda i: (0, i), lambda i: (0, i)
    return pl.pallas_call(
        kernel,
        grid=(grid,),
        in_specs=[pl.BlockSpec((tokens, step), left_map), pl.BlockSpec((tokens, step), right_map)],
        out_specs=pl.BlockSpec((step, step), out_map),
        out_shape=jax.ShapeDtypeStruct((rows, columns), bf16),
        compiler_params=params(),
        name="weight_grad",
    )(left, right)


def attention_back_call(x, q, k, v, gc, ga, stat_l, stat_d, w_qkv):
    count, length, width = x.shape
    block = (None, length, width)

    def kernel(x_ref, q_ref, k_ref, v_ref, gc_ref, ga_ref, l_ref, d_ref, w_ref, gx_ref, gw_ref, sums_ref, kt, gqt, gq, gk, gv, total):
        step = pl.program_id(0)

        @pl.when(step == 0)
        def _():
            sums_ref[...] = jnp.zeros_like(sums_ref)
            total[...] = jnp.zeros_like(total)

        attend_back(q_ref, k_ref, v_ref, gc_ref, l_ref, d_ref, gq, gk, gv, kt, gqt)
        sums_ref[B_QUERY : B_QUERY + 1, :] += column_sum(gq[...])
        sums_ref[B_VALUE : B_VALUE + 1, :] += column_sum(gv[...])
        grad = ga_ref[...].astype(f32)
        x = x_ref[...]
        for i, ref in enumerate((gq, gk, gv)):
            at = slice(i * width, (i + 1) * width)
            grad = grad + mul(ref[...], w_ref[:, at], NT)
            total[:, at] += mul(x, ref[...], TN)
        gx_ref[...] = grad.astype(bf16)

        @pl.when(step == count - 1)
        def _():
            gw_ref[...] = total[...].astype(bf16)

    seq_scratch = pltpu.VMEM((length, width), bf16)
    return pl.pallas_call(
        kernel,
        grid=(count,),
        in_specs=[spec(block)] * 6 + [spec((None, STAT_ROWS, length))] * 2 + [whole_vmem()],
        out_specs=[spec(block), spec((width, 3 * width), False), spec((16, width), False)],
        out_shape=[
            jax.ShapeDtypeStruct(x.shape, bf16),
            jax.ShapeDtypeStruct((width, 3 * width), bf16),
            jax.ShapeDtypeStruct((16, width), f32),
        ],
        scratch_shapes=[pltpu.VMEM((width, length), bf16)] * 2 + [seq_scratch] * 3 + [pltpu.VMEM((width, 3 * width), f32)],
        compiler_params=params(),
        name="attention_back",
    )(x, q, k, v, gc, ga, stat_l, stat_d, w_qkv)


def pack_shard(w_query, w_key, w_value, w_out, w_inner, w_outer, vectors):
    width = w_query.shape[1]
    inner_parts = [w_inner[:, i : i + width] for i in range(0, w_inner.shape[1], width)]
    small = jnp.concatenate(vectors)
    body_rows = sum(part.shape[0] for part in (w_query, w_key, w_value, w_out, w_outer, *inner_parts))
    rows = -(-(body_rows + 1) // 16) * 16
    tail = jnp.zeros(((rows - body_rows) * width,), small.dtype).at[: small.shape[0]].set(small)
    return jnp.concatenate(
        [w_query, w_key, w_value, w_out, *inner_parts, w_outer, tail.reshape(-1, width)]
    )


def vec_table(small, vec_names_sizes):
    rows, at = [], 0
    for size in vec_names_sizes:
        rows.append(small[:, at : at + size].reshape(-1))
        at += size
    return rows


def body(
    tokens,
    span_mask,
    cotangent,
    w_query,
    b_query,
    w_key,
    w_value,
    b_value,
    w_out,
    b_out,
    gain_first,
    bias_first,
    w_inner,
    b_inner,
    w_outer,
    b_outer,
    gain_second,
    bias_second,
):
    rows, stretch, width = tokens.shape
    inner = w_inner.shape[1]
    part = w_query.shape[0]
    outer_part = w_outer.shape[0]
    vectors = (b_query, b_value, b_out, gain_first, bias_first, b_outer, gain_second, bias_second, b_inner)
    sizes = [vector.shape[0] for vector in vectors]

    packed = pack_shard(w_query, w_key, w_value, w_out, w_inner, w_outer, vectors)
    shard_rows = packed.shape[0]
    gathered = lax.all_gather(packed, "batch", axis=0)
    chunks = inner // width

    def weight(at, count):
        return gathered[:, at : at + count].reshape(-1, width)

    squares = [weight(i * part, part) for i in range(4 + chunks)]
    w_qkv = jnp.concatenate(squares[:3], 1)
    w_out_all = squares[3]
    w_inner_all = jnp.concatenate(squares[4:], 1)
    outer_at = (4 + chunks) * part
    w_outer_all = weight(outer_at, outer_part)
    small = gathered[:, outer_at + outer_part :].reshape(gathered.shape[0], -1)
    vec = jnp.concatenate(vec_table(small, sizes)).reshape(-1, width).astype(f32)
    vec = jnp.concatenate([vec, jnp.zeros((16 - vec.shape[0], width), f32)])

    masked = cotangent * span_mask[..., None].astype(bf16)
    swap = functools.partial(lax.all_to_all, axis_name="blk", tiled=True)
    x = swap(tokens, split_axis=0, concat_axis=1)
    cot = swap(masked, split_axis=0, concat_axis=1)

    q, k, v, cb, stat_l = attention_call(x, w_qkv, vec)
    out, mid, gf, ga, gc, stat_d, hidden, gu, sums_ffn = feed_forward_call(
        x, cb, cot, w_out_all, w_inner_all, w_outer_all, vec
    )
    gx, gw_qkv, sums_att = attention_back_call(x, q, k, v, gc, ga, stat_l, stat_d, w_qkv)
    output = swap(out, split_axis=1, concat_axis=0)
    grad_tokens = swap(gx, split_axis=1, concat_axis=0)

    def flat(values):
        return values.reshape(-1, values.shape[-1])

    gw_out = weight_grad_call(flat(cb), flat(ga), False)
    gw_inner = weight_grad_call(flat(mid), flat(gu), False)
    gw_outer = weight_grad_call(flat(hidden), flat(gf), True)

    devices = gathered.shape[0]
    sums = sums_ffn + sums_att
    small_sums = [sums[i].reshape(devices, -1) for i in range(B_INNER)]
    small_sums.append(sums[B_INNER : B_INNER + chunks].reshape(devices, -1))
    tail = jnp.concatenate(small_sums, 1).astype(bf16)
    tail = jnp.pad(tail, ((0, 0), (0, (shard_rows - outer_at - outer_part) * width - tail.shape[1])))
    pieces = [gw_qkv[:, i * width : (i + 1) * width].reshape(devices, part, width) for i in range(3)]
    pieces.append(gw_out.reshape(devices, part, width))
    pieces += [gw_inner[:, i * width : (i + 1) * width].reshape(devices, part, width) for i in range(chunks)]
    pieces.append(gw_outer.reshape(devices, outer_part, width))
    pieces.append(tail.reshape(devices, -1, width))
    grads = jnp.concatenate(pieces, 1)
    share = lax.psum_scatter(grads, "batch", scatter_dimension=0, tiled=False)
    share = lax.psum(share, "blk").astype(f32)
    square = [share[i * part : (i + 1) * part] for i in range(4 + chunks)]
    share_small = share[outer_at + outer_part :].reshape(-1)
    small_out, at = [], 0
    for size in sizes:
        small_out.append(share_small[at : at + size])
        at += size
    (g_b_query, g_b_value, g_b_out, g_gain_1, g_bias_1, g_b_outer, g_gain_2, g_bias_2, g_b_inner) = small_out
    return (
        output,
        grad_tokens,
        square[0],
        g_b_query,
        square[1],
        square[2],
        g_b_value,
        square[3],
        g_b_out,
        g_gain_1,
        g_bias_1,
        jnp.concatenate(square[4:], 1),
        g_b_inner,
        share[outer_at : outer_at + outer_part],
        g_b_outer,
        g_gain_2,
        g_bias_2,
    )


def solution(mesh):
    block = P("batch", "blk", None)
    matrix, vector = P("batch", None), P("batch")
    weights = (
        matrix, vector, matrix, matrix, vector, matrix, vector, vector, vector, matrix, vector, matrix, vector, vector, vector,
    )
    return jax.shard_map(
        body,
        mesh=mesh,
        in_specs=(block, P("batch", "blk"), block) + weights,
        out_specs=(block, block) + weights,
        check_vma=False,
    )
```

time: 1230 us -> 611 us (0.50)
  matrix products: 383 us -> 0 us
  waiting for transfers between devices: 500 us -> 255 us
  Pallas kernels: 0 us -> 198 us
  blocking collectives: 136 us -> 0 us
  other arithmetic: 65 us -> 14 us
  starting transfers between devices: 0.68 us -> 18.9 us
    dot_general x24 -> x0, matrix products: 383 us -> none  [the longest x6 75.9 us: back_product(): lax.dot_general(grad, matrix, (((1,), (1,)), ((), ())), preferred_element...]
    all_gather x10 -> x1, waiting for transfers between devices: 236 us -> 29.5 us  [body(): gathered = lax.all_gather(packed, 'batch', axis=0)]
    pallas_call x0 -> x6, Pallas kernels: none -> 198 us  [the longest x1 69.4 us: feed_forward_call(): pl.pallas_call(kernel, grid=(count,), in_specs=[spec(block)] * 3 + [whole...]
    reduce_scatter x3 -> x1, waiting for transfers between devices: 216 us -> 95.1 us  [body(): share = lax.psum_scatter(grads, 'batch', scatter_dimension=0, tiled=False)]
    unnamed x2 -> x0, blocking collectives: 118 us -> none
    all_to_all x0 -> x4, waiting for transfers between devices: none -> 97.7 us  [the longest x1 34 us: body(): cot = swap(masked, split_axis=0, concat_axis=1)]
    unnamed x20 -> x3, waiting for transfers between devices: 48.1 us -> 0.05 us
    reduce_sum x7 -> x0, other arithmetic: 38.7 us -> none  [the longest x1 21.2 us: body(): total = jnp.sum(weights, -1)]
  transfers between devices with their start and end apart: 17 -> 7, of which waited for: 12 -> 6; matrix products, arithmetic and copies ran while one was open for 37% -> 4% of each run, Pallas kernels for 0% -> 0%
where the time goes in v1:
time: 611 us; the launch traced here: 604 us
  waiting for transfers between devices  255 us (42%)
  Pallas kernels  198 us (32%)
  local copies, waits for them, and re-layouts  104 us (17%)
  starting transfers between devices  18.9 us (3%)
  between operations  14.4 us (2%)
  other arithmetic  14 us (2%)
    reduce_scatter x1, waiting for transfers between devices, body(): share = lax.psum_scatter(grads, 'batch', scatter_dimension=0, tiled=False)  95.1 us
    pallas_call x1, Pallas kernels, feed_forward_call(): pl.pallas_call(kernel, grid=(count,), in_specs=[spec(block)] * 3 + [whole...  69.4 us
    pallas_call x1, Pallas kernels, attention_back_call(): pl.pallas_call(kernel, grid=(count,), in_specs=[spec(block)] * 6 + [spec(...  59.1 us
    unnamed x48, local copies, waits for them, and re-layouts  36.9 us
    pallas_call x3, Pallas kernels, weight_grad_call(): pl.pallas_call(kernel, grid=(grid,), in_specs=[pl.BlockSpec((tokens, step...  35.9 us
    all_to_all x1, waiting for transfers between devices, body(): cot = swap(masked, split_axis=0, concat_axis=1)  34 us
    all_to_all x1, waiting for transfers between devices, body(): x = swap(tokens, split_axis=0, concat_axis=1)  33.4 us
    pallas_call x1, Pallas kernels, attention_call(): pl.pallas_call(kernel, grid=(count,), in_specs=[spec(block), whole_vmem()...  33.3 us
  transfers between devices with their start and end apart: 7, of which 6 were waited for; matrix products, arithmetic and copies ran while one was open for 4% of the time, Pallas kernels for 0%

profile of v1, /device:TPU:0, one launch (start us, length us, event | category | flops | bytes accessed | tf_op | source)
XLA Modules:
  0.0 604.2 jit_solution(2963374496671577998)
XLA Ops:
  7.2 6.1 %concatenate.32 = bf16[576]{0:T(1024)(128)(2,1)S(1)} concatenate(bf16[48]{0:T(256)(128)(2,1)} %param.24, bf16[48]{0:T(256)(128)(2,1)} %param.27, bf16[48]{0:T(256)(128)(2,1)} %param.29, bf16[48]{0:T(256)(128)(2,1)} %param.30, bf16[48]{0:T(256)(128)(2,1)} %param.31, bf16[48]{0:T(256)(128)(2,1)} %param.35, bf16[48]{0:T(256)(128)(2,1)} %param.36, bf16[48]{0:T(256)(128)(2,1)} %param.37, ...), dimensions={0} | concatenate | bytes 2304 | tf_op jit(solution)/shard_map/concatenate | solution.py:315
  22.5 4.2 all-to-all-start
  26.7 3.9 broadcast_multiply_fusion
  30.6 33.4 %all-to-all-done = bf16[8,256,768]{2,1,0:T(8,128)(2,1)S(1)} async-done(((bf16[8,256,768]{2,1,0:T(8,128)(2,1)}), bf16[8,256,768]{2,1,0:T(8,128)(2,1)S(1)}, u32[]{:S(2)}, u32[]{:S(2)}) %all-to-all-start) | async-done | bytes 3145760 | tf_op jit(solution)/shard_map/all_to_all | solution.py:379
  64.0 5.2 all-to-all-start.1
  69.3 1.9 copy.39
  71.2 34.0 %all-to-all-done.1 = bf16[8,256,768]{2,1,0:T(8,128)(2,1)} async-done(((bf16[8,256,768]{2,1,0:T(8,128)(2,1)}), bf16[8,256,768]{2,1,0:T(8,128)(2,1)}, u32[]{:S(2)}, u32[]{:S(2)}) %all-to-all-start.1) | async-done | bytes 3145760 | tf_op jit(solution)/shard_map/all_to_all | solution.py:380
  105.2 3.7 copy.40
  108.9 29.5 %all-gather.3.cloned.1.call-done = bf16[9472,768]{1,0:T(8,128)(2,1)} async-done(((bf16[592,768]{1,0:T(8,128)(2,1)}), bf16[9472,768]{1,0:T(8,128)(2,1)}) %all-gather.3.cloned.1.call-update) | async-done | bytes 14549008 | tf_op jit(solution)/shard_map/all_gather | solution.py:361
  140.2 5.0 slice.270
  145.2 6.4 %fusion = (bf16[16,48,768]{2,1,0:T(8,128)(2,1)S(1)}, bf16[16,48,768]{2,1,0:T(8,128)(2,1)S(1)}, bf16[16,48,768]{2,1,0:T(8,128)(2,1)S(1)}, bf16[16,48,768]{2,1,0:T...) fusion(bf16[16,592,768]{2,1,0:T(8,128)(2,1)} %bitcast.55), kind=kLoop, calls=%fused_computation.35 | loop fusion | bytes 18874368 | tf_op jit(solution)/shard_map/slice | solution.py:365
  153.2 1.4 reshape.186
  154.6 1.4 reshape.185
  155.9 1.4 reshape.184
  161.3 1.4 dynamic-update-slice.12
  162.8 1.4 dynamic-update-slice.13
  164.2 1.4 dynamic-update-slice.14
  165.6 1.4 dynamic-update-slice.15
  167.1 1.4 dynamic-update-slice.16
  168.5 1.4 dynamic-update-slice.17
  169.9 1.4 dynamic-update-slice.18
  171.3 1.4 dynamic-update-slice.19
  173.3 1.4 convert_element_type.14
  174.7 1.4 pad_convert_fusion.vec_ref
  176.1 3.3 pad_maximum_fusion.1.w_ref
  179.4 33.3 %attention.1 = (bf16[4,512,768]{2,1,0:T(8,128)(2,1)}, bf16[4,512,768]{2,1,0:T(8,128)(2,1)}, bf16[4,512,768]{2,1,0:T(8,128)(2,1)}, bf16[4,512,768]{2,1,0:T(8,128)(2,1)}, f32[4,16,512]{2,1,0:T(8,128)}) custom-call(bf16[4,512,768]{2,1,0:T(8,128)(2,1)} %bitcast.46, bf16[768,2304]{1,0:T(8,128)(2,1)} %pad_maximum_fusion.1.w_ref, f32[16,768]{1,0:T(8,128)} %pad_convert_fusion.vec_ref), custom_call_target="tpu_custom_call" | custom-call | tf_op jit(solution)/shard_map/attention/pallas_call | solution.py:199
  212.7 3.8 pad_maximum_fusion.wi
  216.5 69.4 %feed_forward.1 = (bf16[4,512,768]{2,1,0:T(8,128)(2,1)}, bf16[4,512,768]{2,1,0:T(8,128)(2,1)}, bf16[4,512,768]{2,1,0:T(8,128)(2,1)}, bf16[4,512,768]{2,1,0:T(8,1...) custom-call(bf16[4,512,768]{2,1,0:T(8,128)(2,1)} %bitcast.47, ...), custom_call_target="tpu_custom_call" | custom-call | tf_op jit(solution)/shard_map/feed_forward/pallas_call | solution.py:227
  285.8 59.1 %attention_back.1 = (bf16[4,512,768]{2,1,0:T(8,128)(2,1)}, bf16[768,2304]{1,0:T(8,128)(2,1)}, f32[16,768]{1,0:T(8,128)}) custom-call(bf16[4,512,768]{2,1,0:T(8,128)(2,1)} %bitcast.48, bf16[4,512,768]{2,1,0:T(8,128)(2,1)} %get-tuple-element.48.q_ref, bf16[4,512,768]{2,1,0:T(8,128)(2,1)} %get-tuple-element.49.k_ref, ...), custom_call_target="tpu_custom_call" | custom-call | tf_op jit(solution)/shard_map/attention_back/pallas_call | solution.py:296
  346.9 3.9 fusion.2
  350.8 14.7 %weight_grad.4 = bf16[768,3072]{1,0:T(8,128)(2,1)} custom-call(bf16[2048,768]{1,0:T(8,128)(2,1)} %bitcast.80, bf16[2048,3072]{1,0:T(8,128)(2,1)} %bitcast.57), custom_call_target="tpu_custom_call" | custom-call | tf_op jit(solution)/shard_map/weight_grad/pallas_call | solution.py:257
  365.5 3.8 fusion.1
  370.4 6.5 %weight_grad.3 = bf16[768,768]{1,0:T(8,128)(2,1)} custom-call(bf16[2048,768]{1,0:T(8,128)(2,1)} %bitcast.60, bf16[2048,768]{1,0:T(8,128)(2,1)} %bitcast.61), custom_call_target="tpu_custom_call" | custom-call | tf_op jit(solution)/shard_map/weight_grad/pallas_call | solution.py:257
  376.9 14.8 %weight_grad.5 = bf16[3072,768]{1,0:T(8,128)(2,1)} custom-call(bf16[2048,3072]{1,0:T(8,128)(2,1)} %bitcast.56, bf16[2048,768]{1,0:T(8,128)(2,1)} %bitcast.79), custom_call_target="tpu_custom_call" | custom-call | tf_op jit(solution)/shard_map/weight_grad/pallas_call | solution.py:257
  391.7 2.6 constant_dynamic-update-slice_fusion.14
  395.4 2.4 constant_dynamic-update-slice_fusion.12
  402.2 2.6 constant_dynamic-update-slice_fusion.7
  405.7 1.9 copy-done.4
  407.6 4.1 copy.43
  411.7 4.1 all-to-all-start.3
  415.8 6.5 %copy.41 = bf16[4,512,768]{2,0,1:T(4,128)(2,1)} copy(bf16[4,512,768]{2,1,0:T(8,128)(2,1)} %get-tuple-element.47) | data formatting | bytes 6291456 | tf_op jit(solution)/shard_map/feed_forward/pallas_call | solution.py:227
  422.3 30.3 %all-to-all-done.3 = bf16[4,512,768]{2,0,1:T(4,128)(2,1)S(1)} async-done(((bf16[4,512,768]{2,0,1:T(4,128)(2,1)}), bf16[4,512,768]{2,0,1:T(4,128)(2,1)S(1)}, u32[]{:S(2)}, u32[]{:S(2)}) %all-to-all-start.3) | async-done | bytes 3145760 | tf_op jit(solution)/shard_map/all_to_all | solution.py:388
  452.6 5.2 all-to-all-start.2
  457.9 95.1 %reduce-scatter.2.cloned.1.call-done = bf16[1,592,768]{2,1,0:T(8,128)(2,1)} async-done(((bf16[16,592,768]{2,1,0:T(8,128)(2,1)}), bf16[1,592,768]{2,1,0:T(8,128)(2,1)}) %reduce-scatter.2.cloned.1.call-update) | async-done | bytes 909328 | tf_op jit(solution)/shard_map/reduce_scatter | solution.py:409
  553.0 2.1 copy.44
  555.1 4.0 copy.42
  559.0 32.5 %all-reduce.5.cloned.1.call-done = bf16[592,768]{1,0:T(8,128)(2,1)} async-done(((bf16[592,768]{1,0:T(8,128)(2,1)}), bf16[592,768]{1,0:T(8,128)(2,1)}) %all-reduce.5.cloned.1.call-update) | async-done | bytes 909328 | tf_op jit(solution)/shard_map/psum | solution.py:410
  593.5 2.0 fusion.3
  (80 shorter events, 30.6 us)
Async XLA Ops:
  7.2 131.2 %all-gather.3.cloned.1.call-start = ((), (), s32[]{:S(2)}) async-start(), calls=%async_computation.7 | async-start | bytes 15458304 | tf_op jit(solution)/shard_map/all_gather | solution.py:361
  21.5 1.0 copy-start.5
  22.5 4.2 copy-start.7
  22.5 41.5 %all-to-all-start = ((bf16[8,256,768]{2,1,0:T(8,128)(2,1)}), bf16[8,256,768]{2,1,0:T(8,128)(2,1)S(1)}, u32[]{:S(2)}, u32[]{:S(2)}) async-start(bf16[8,256,768]{2,1,0:T(8,128)(2,1)} %param.20), calls=%async_computation | async-start | bytes 6291456 | tf_op jit(solution)/shard_map/all_to_all | solution.py:379
  64.0 41.2 %all-to-all-start.1 = ((bf16[8,256,768]{2,1,0:T(8,128)(2,1)}), bf16[8,256,768]{2,1,0:T(8,128)(2,1)}, u32[]{:S(2)}, u32[]{:S(2)}) async-start(bf16[8,256,768]{2,1,0:T(8,128)(2,1)} %broadcast_multiply_fusion), calls=%async_computation.1 | async-start | bytes 6291456 | tf_op jit(solution)/shard_map/all_to_all | solution.py:380
  69.2 483.8 %reduce-scatter.2.cloned.1.call-start = ((), (), s32[]{:S(2)}) async-start(), calls=%async_computation.5 | async-start | bytes 15458304 | tf_op jit(solution)/shard_map/reduce_scatter | solution.py:409
  285.8 59.1 %copy-start.6 = (f32[16,768]{1,0:T(8,128)S(1)}, f32[16,768]{1,0:T(8,128)}, u32[]{:S(2)}) copy-start(f32[16,768]{1,0:T(8,128)} %get-tuple-element.61) | copy-start | bytes 147460
  365.5 3.8 copy-start.2
  391.7 2.6 copy-start.1
  391.7 6.1 %copy-start = (bf16[768,768]{1,0:T(8,128)(2,1)S(1)}, bf16[768,768]{1,0:T(8,128)(2,1)}, u32[]{:S(2)}) copy-start(bf16[768,768]{1,0:T(8,128)(2,1)} %get-tuple-element.82) | copy-start | bytes 3538948
  391.7 10.5 %slice-start = ((s8[4718592]{0:T(1024)(128)(4,1)}), s8[4194304]{0:T(1024)(128)(4,1)S(1)}, s32[]{:S(2)}) async-start(s8[4718592]{0:T(1024)(128)(4,1)} %bitcast.49), calls=%async_computation.8 | async-start | bytes 8388608
  397.8 4.5 slice-start.1
  405.7 1.9 copy-start.4
  411.7 40.9 %all-to-all-start.3 = ((bf16[4,512,768]{2,0,1:T(4,128)(2,1)}), bf16[4,512,768]{2,0,1:T(4,128)(2,1)S(1)}, u32[]{:S(2)}, u32[]{:S(2)}) async-start(bf16[4,512,768]{2,0,1:T(4,128)(2,1)} %copy.43), calls=%async_computation.3 | async-start | bytes 6291456 | tf_op jit(solution)/shard_map/all_to_all | solution.py:388
  452.6 102.5 %all-to-all-start.2 = ((bf16[4,512,768]{2,0,1:T(4,128)(2,1)}), bf16[4,512,768]{2,0,1:T(4,128)(2,1)}, u32[]{:S(2)}, u32[]{:S(2)}) async-start(bf16[4,512,768]{2,0,1:T(4,128)(2,1)} %copy.41), calls=%async_computation.2 | async-start | bytes 6291456 | tf_op jit(solution)/shard_map/all_to_all | solution.py:387
  457.9 133.7 %all-reduce.5.cloned.1.call-start = ((), (), s32[]{:S(2)}) async-start(), calls=%async_computation.6 | async-start | bytes 1818624 | tf_op jit(solution)/shard_map/psum | solution.py:410
  591.5 4.9 copy-start.3
Sparse Core Ops, SparseCore 0:
  22.6 115.7 all-gather.2
  405.8 147.1 reduce-scatter.1
  555.4 36.0 all-reduce.4

commit v2 on v1

--- a/solution.py
+++ b/solution.py
@@ -69,9 +69,8 @@
     v_ref[...] = (mul(x, w_ref[:, 2 * width :]) + row(vec_ref, B_VALUE)).astype(bf16)
 
 
-def attend(q_ref, k_ref, v_ref, c_ref, l_ref, stat):
-    length = q_ref.shape[0]
-    lane = lax.broadcasted_iota(jnp.int32, (length, 128), 1)
+def attend_pairs(q_ref, k_ref, v_ref, c_ref, stat, first, end):
+    lane = lax.broadcasted_iota(jnp.int32, stat.shape, 1)
 
     def pair(p, carry):
         at = pair_at(p)
@@ -88,8 +87,12 @@
         c_ref[:, at] = context.astype(bf16)
         return carry
 
+    lax.fori_loop(first, end, pair, 0, unroll=3)
+
+
+def attend(q_ref, k_ref, v_ref, c_ref, l_ref, stat):
     stat[...] = jnp.zeros_like(stat)
-    lax.fori_loop(0, HEADS // 2, pair, 0, unroll=2)
+    attend_pairs(q_ref, k_ref, v_ref, c_ref, stat, 0, HEADS // 2)
     l_ref[...] = stat[...].T[:STAT_ROWS]
 
 
@@ -309,6 +312,388 @@
     )(x, q, k, v, gc, ga, stat_l, stat_d, w_qkv)
 
 
+def forward_call(tokens, span_mask, cotangent, w_query, w_key, w_value, w_out, w_inner, w_outer, table, sizes):
+    depth_z, depth_y, cores = sizes
+    rows, stretch, width = tokens.shape
+    inner = w_inner.shape[1]
+    part, outer_part = w_query.shape[0], w_outer.shape[0]
+    devices = depth_z * depth_y * cores
+    count, length = rows // 2, 2 * stretch
+    chunks = inner // width
+    qkv_width, mid_width = 3 * width, width + inner
+    last = depth_z - 1
+    ARRAYS = 4
+
+    def kernel(
+        tokens_ref, mask_ref, cot_ref, wq_in, wk_in, wv_in, wo_in, wi_in, wu_in, table_in,
+        x_out, q_out, k_out, v_out, cb_out, l_out, o_out, mid_out, gf_out, ga_out, gc_out, d_out, h_out, gu_out,
+        sums_out, w_qkv_out,
+        w_qkv, w_mid, w_up, tables, vec, x_all, cot_all, cot_away, cb_all, q_s, k_s, v_s, l_s, stat, o_s, mid_s, gf_s,
+        ga_s, gc_s, d_s, h_s, gu_s,
+        up_send, down_send, z_recv, y_send, y_recv, c_send, c_recv, t_send, t_recv, g_send, g_recv, in_sem, out_sem,
+    ):
+        b, k = lax.axis_index("batch"), lax.axis_index("blk")
+        z, y, c = b // (depth_y * cores), (b // cores) % depth_y, b % cores
+
+        def at(z_, y_, c_):
+            return (z_ * depth_y + y_) * cores + c_
+
+        barrier = pltpu.get_barrier_semaphore()
+
+        def greet(device):
+            pl.semaphore_signal(barrier, inc=1, device_id=device, device_id_type=pl.DeviceIdType.MESH)
+
+        greet((b, 1 - k))
+        greet((at(z, 1 - y, c), k))
+        greet((at(z, y, 1 - c), k))
+
+        @pl.when(z < last)
+        def _():
+            greet((at(z + 1, y, c), k))
+
+        @pl.when(z > 0)
+        def _():
+            greet((at(z - 1, y, c), k))
+
+        shard = pl.ds(b * part, part)
+        mine = pl.ds(pl.multiple_of(k * stretch, stretch), stretch)
+        loads = [
+            pltpu.make_async_copy(wq_in, w_qkv.at[shard, 0:width], in_sem.at[0]),
+            pltpu.make_async_copy(wk_in, w_qkv.at[shard, width : 2 * width], in_sem.at[1]),
+            pltpu.make_async_copy(wv_in, w_qkv.at[shard, 2 * width : 3 * width], in_sem.at[2]),
+            pltpu.make_async_copy(wo_in, w_mid.at[shard, 0:width], in_sem.at[3]),
+            pltpu.make_async_copy(wi_in, w_mid.at[shard, width:mid_width], in_sem.at[4]),
+            pltpu.make_async_copy(wu_in, w_up.at[pl.ds(b * outer_part, outer_part)], in_sem.at[5]),
+            pltpu.make_async_copy(cot_ref.at[pl.ds(k * count, count)], cot_all.at[:, mine], in_sem.at[6]),
+            pltpu.make_async_copy(cot_ref.at[pl.ds((1 - k) * count, count)], cot_away, in_sem.at[7]),
+            pltpu.make_async_copy(tokens_ref.at[pl.ds(k * count, count)], x_all.at[:, mine], in_sem.at[8]),
+        ]
+        for load in loads:
+            load.start()
+
+        raw = table_in[...]
+        rolled = pltpu.roll(raw, b * part, 1)
+        wide = pltpu.roll(raw[B_INNER : B_INNER + 1, :], (b % (devices // chunks)) * outer_part, 1)
+        line = lax.broadcasted_iota(jnp.int32, raw.shape, 0)
+        own_table = jnp.where(line < B_INNER, rolled, 0.0)
+        own_table = jnp.where(line == B_INNER + b // (devices // chunks), wide, own_table)
+        tables[b] = own_table.astype(bf16)
+
+        def piece(array, z_, y_, c_):
+            d = at(z_, y_, c_)
+            if array == 0:
+                return w_qkv.at[pl.ds(d * part, part)]
+            if array == 1:
+                return tables.at[d]
+            if array == 2:
+                return w_mid.at[pl.ds(d * part, part)]
+            return w_up.at[pl.ds(d * outer_part, outer_part)]
+
+        def remote(ref, device, send, recv):
+            return pltpu.make_async_remote_copy(
+                src_ref=ref, dst_ref=ref, send_sem=send, recv_sem=recv, device_id=device, device_id_type=pl.DeviceIdType.MESH
+            )
+
+        def up(a, zs):
+            return remote(piece(a, zs, y, c), (at(z + 1, y, c), k), up_send.at[a, zs], z_recv.at[a, zs])
+
+        def down(a, zs):
+            return remote(piece(a, zs, y, c), (at(z - 1, y, c), k), down_send.at[a, zs], z_recv.at[a, zs])
+
+        def across(a, zs):
+            return remote(piece(a, zs, y, c), (at(z, 1 - y, c), k), y_send.at[a, zs], y_recv.at[a, zs])
+
+        def core(a, zs, ys):
+            i = zs * depth_y + ys
+            return remote(piece(a, zs, ys, c), (at(z, y, 1 - c), k), c_send.at[a, i], c_recv.at[a, i])
+
+        def arrived(ref, sem):
+            remote(ref, (b, 1 - k), sem, sem).wait_recv()
+
+        def begin(a):
+            @pl.when(z < last)
+            def _():
+                up(a, z).start()
+
+            @pl.when(z > 0)
+            def _():
+                down(a, z).start()
+
+            across(a, z).start()
+            core(a, z, y).start()
+
+        def hop(a, step):
+            @pl.when(z >= step)
+            def _():
+                zs = z - step
+                arrived(piece(a, zs, y, c), z_recv.at[a, zs])
+
+                @pl.when(z < last)
+                def _():
+                    up(a, zs).start()
+
+                across(a, zs).start()
+                core(a, zs, y).start()
+
+            @pl.when(z + step <= last)
+            def _():
+                zs = z + step
+                arrived(piece(a, zs, y, c), z_recv.at[a, zs])
+
+                @pl.when(z > 0)
+                def _():
+                    down(a, zs).start()
+
+                across(a, zs).start()
+                core(a, zs, y).start()
+
+        def relay(a, step):
+            def one(zs):
+                arrived(piece(a, zs, 1 - y, c), y_recv.at[a, zs])
+                core(a, zs, 1 - y).start()
+
+            if step == 0:
+                one(z)
+                return
+
+            @pl.when(z >= step)
+            def _():
+                one(z - step)
+
+            @pl.when(z + step <= last)
+            def _():
+                one(z + step)
+
+        def complete(a):
+            for zs in range(depth_z):
+                for ys in range(depth_y):
+                    arrived(piece(a, zs, ys, 1 - c), c_recv.at[a, zs * depth_y + ys])
+
+        def sent(a):
+            for zs in range(depth_z):
+                @pl.when((z < last) & (zs <= z))
+                def _():
+                    up(a, zs).wait_send()
+
+                @pl.when((z > 0) & (zs >= z))
+                def _():
+                    down(a, zs).wait_send()
+
+                across(a, zs).wait_send()
+                for ys in range(depth_y):
+                    core(a, zs, ys).wait_send()
+
+        def token_copy(s):
+            return pltpu.make_async_remote_copy(
+                src_ref=tokens_ref.at[(1 - k) * count + s],
+                dst_ref=x_all.at[s, mine],
+                send_sem=t_send.at[s],
+                recv_sem=t_recv.at[s],
+                device_id=(b, 1 - k),
+                device_id_type=pl.DeviceIdType.MESH,
+            )
+
+        def grad_copy(s):
+            return pltpu.make_async_remote_copy(
+                src_ref=cot_away.at[s],
+                dst_ref=cot_all.at[s, mine],
+                send_sem=g_send.at[s],
+                recv_sem=g_recv.at[s],
+                device_id=(b, 1 - k),
+                device_id_type=pl.DeviceIdType.MESH,
+            )
+
+        def put(i, src, dst):
+            return pltpu.make_async_copy(src, dst, out_sem.at[i])
+
+        partners = 3 + (z < last).astype(jnp.int32) + (z > 0).astype(jnp.int32)
+        pl.semaphore_wait(barrier, partners)
+        token_copy(0).start()
+        begin(1)
+        for i in range(3):
+            loads[i].wait()
+        begin(0)
+        token_copy(1).start()
+
+        for i in (6, 7):
+            loads[i].wait()
+        mask = mask_ref[...].astype(f32)
+        own, away = jnp.where(k == 0, mask[:count], mask[count:]), jnp.where(k == 0, mask[count:], mask[:count])
+        columns = jnp.concatenate([own, away], 0).T
+        for s in range(count):
+            cot_all[s, mine, :] = (cot_all[s, mine, :].astype(f32) * columns[:, s : s + 1]).astype(bf16)
+            cot_away[s] = (cot_away[s].astype(f32) * columns[:, count + s : count + s + 1]).astype(bf16)
+
+        for i in (3, 4, 5, 8):
+            loads[i].wait()
+        relay(0, 0)
+        relay(1, 0)
+        for step in range(1, depth_z):
+            for a in (0, 1):
+                hop(a, step)
+        begin(2)
+        for step in range(1, depth_z):
+            for a in (0, 1):
+                relay(a, step)
+        complete(0)
+        complete(1)
+        vec[...] = jnp.sum(tables[...].astype(f32), 0)
+        save_w = put(0, w_qkv, w_qkv_out)
+        save_w.start()
+
+        plan = {
+            (0, 0): [],
+            (0, 1): [lambda: hop(2, 1)],
+            (0, 2): [lambda: relay(2, 0)],
+            (1, 0): [lambda: hop(2, 2)],
+            (1, 1): [lambda: relay(2, 1)],
+            (1, 2): [lambda: hop(2, 3), lambda: begin(3)],
+            (2, 0): [lambda: relay(2, 2)],
+            (2, 1): [lambda: hop(3, 1)],
+            (2, 2): [],
+            (3, 0): [lambda: hop(3, 2), lambda: relay(2, 3)],
+            (3, 1): [lambda: relay(3, 0)],
+            (3, 2): [lambda: hop(3, 3)],
+        }
+
+        def pump(s, slot):
+            for (when, where), steps in plan.items():
+                if where == slot and steps:
+                    @pl.when(s == when)
+                    def _():
+                        for step in steps:
+                            step()
+
+        def first(s, carry):
+            arrived(x_all.at[s, pl.ds(pl.multiple_of((1 - k) * stretch, stretch), stretch)], t_recv.at[s])
+
+            @pl.when(s + 2 < count)
+            def _():
+                token_copy(s + 2).start()
+
+            @pl.when(s + 2 >= count)
+            def _():
+                grad_copy(s + 2 - count).start()
+
+            saves = [
+                put(1, x_all.at[s], x_out.at[s]),
+                put(2, q_s, q_out.at[s]),
+                put(3, k_s, k_out.at[s]),
+                put(4, v_s, v_out.at[s]),
+                put(5, cb_all.at[s], cb_out.at[s]),
+                put(6, l_s, l_out.at[s]),
+            ]
+
+            @pl.when(s > 0)
+            def _():
+                for save in saves:
+                    save.wait()
+
+            project(x_all[s], w_qkv, vec, q_s, k_s, v_s)
+            for save in saves[:4]:
+                save.start()
+            pump(s, 0)
+            stat[...] = jnp.zeros_like(stat)
+            attend_pairs(q_s, k_s, v_s, cb_all.at[s], stat, 0, HEADS // 4)
+            pump(s, 1)
+            attend_pairs(q_s, k_s, v_s, cb_all.at[s], stat, HEADS // 4, HEADS // 2)
+            l_s[...] = stat[...].T[:STAT_ROWS]
+            for save in saves[4:]:
+                save.start()
+            pump(s, 2)
+            return carry
+
+        lax.fori_loop(0, count, first, 0)
+        for i, (src, dst) in enumerate(((x_all.at[0], x_out.at[0]), (q_s, q_out.at[0]), (k_s, k_out.at[0]), (v_s, v_out.at[0]), (cb_all.at[0], cb_out.at[0]), (l_s, l_out.at[0]))):
+            put(i + 1, src, dst).wait()
+        save_w.wait()
+        for step in range(1, depth_z):
+            relay(3, step)
+        complete(2)
+        complete(3)
+
+        sums_out[...] = jnp.zeros_like(sums_out)
+
+        def second(s, carry):
+            arrived(cot_all.at[s, pl.ds(pl.multiple_of((1 - k) * stretch, stretch), stretch)], g_recv.at[s])
+
+            @pl.when(s + 2 < count)
+            def _():
+                grad_copy(s + 2).start()
+
+            saves = [
+                put(i + 1, src, dst.at[s])
+                for i, (src, dst) in enumerate(
+                    (
+                        (o_s, o_out), (mid_s, mid_out), (gf_s, gf_out), (ga_s, ga_out), (gc_s, gc_out), (d_s, d_out),
+                        (h_s, h_out), (gu_s, gu_out),
+                    )
+                )
+            ]
+
+            @pl.when(s > 0)
+            def _():
+                for save in saves:
+                    save.wait()
+
+            feed_forward(
+                x_all[s], cb_all[s], cot_all[s], w_mid.at[:, 0:width], w_mid.at[:, width:mid_width], w_up, vec,
+                o_s, mid_s, gf_s, ga_s, gc_s, d_s, h_s, gu_s, sums_out,
+            )
+            for save in saves:
+                save.start()
+            return carry
+
+        lax.fori_loop(0, count, second, 0)
+        for i, (src, dst) in enumerate(
+            (
+                (o_s, o_out), (mid_s, mid_out), (gf_s, gf_out), (ga_s, ga_out), (gc_s, gc_out), (d_s, d_out),
+                (h_s, h_out), (gu_s, gu_out),
+            )
+        ):
+            put(i + 1, src, dst.at[0]).wait()
+        for s in range(count):
+            token_copy(s).wait_send()
+            grad_copy(s).wait_send()
+        for a in range(ARRAYS):
+            sent(a)
+
+    seq = jax.ShapeDtypeStruct((count, length, width), bf16)
+    seq_wide = jax.ShapeDtypeStruct((count, length, inner), bf16)
+    stat_shape = jax.ShapeDtypeStruct((count, STAT_ROWS, length), f32)
+    hbm = pl.BlockSpec(memory_space=pl.ANY)
+    one = pltpu.VMEM((length, width), bf16)
+    one_wide = pltpu.VMEM((length, inner), bf16)
+    all_seq = pltpu.VMEM((count, length, width), bf16)
+    stat_one = pltpu.VMEM((STAT_ROWS, length), f32)
+    dma = pltpu.SemaphoreType.DMA
+    return pl.pallas_call(
+        kernel,
+        in_specs=[hbm, whole_vmem()] + [hbm] * 7 + [whole_vmem()],
+        out_specs=[hbm] * 14 + [whole_vmem(), hbm],
+        out_shape=[seq] * 5 + [stat_shape] + [seq] * 5 + [stat_shape, seq_wide, seq_wide]
+        + [jax.ShapeDtypeStruct((16, width), f32), jax.ShapeDtypeStruct((width, qkv_width), bf16)],
+        scratch_shapes=[
+            pltpu.VMEM((width, qkv_width), bf16),
+            pltpu.VMEM((width, mid_width), bf16),
+            pltpu.VMEM((inner, width), bf16),
+            pltpu.VMEM((devices, 16, width), bf16),
+            pltpu.VMEM((16, width), f32),
+            all_seq, all_seq,
+            pltpu.VMEM((count, stretch, width), bf16),
+            all_seq,
+            one, one, one, stat_one, pltpu.VMEM((length, 128), f32),
+            one, one, one, one, one, stat_one, one_wide, one_wide,
+            dma((ARRAYS, depth_z)), dma((ARRAYS, depth_z)), dma((ARRAYS, depth_z)),
+            dma((ARRAYS, depth_z)), dma((ARRAYS, depth_z)),
+            dma((ARRAYS, depth_z * depth_y)), dma((ARRAYS, depth_z * depth_y)),
+            dma((count,)), dma((count,)), dma((count,)), dma((count,)), dma((9,)), dma((9,)),
+        ],
+        compiler_params=pltpu.CompilerParams(collective_id=1, has_side_effects=True, vmem_limit_bytes=VMEM_BYTES),
+        name="forward",
+    )(tokens, span_mask, cotangent, w_query, w_key, w_value, w_out, w_inner, w_outer, table)
+
+
 def pack_shard(w_query, w_key, w_value, w_out, w_inner, w_outer, vectors):
     width = w_query.shape[1]
     inner_parts = [w_inner[:, i : i + width] for i in range(0, w_inner.shape[1], width)]
@@ -327,6 +712,26 @@
         rows.append(small[:, at : at + size].reshape(-1))
         at += size
     return rows
+
+
+def gather_weights(w_query, w_key, w_value, w_out, w_inner, w_outer, vectors):
+    part, width = w_query.shape
+    outer_part = w_outer.shape[0]
+    chunks = w_inner.shape[1] // width
+    sizes = [vector.shape[0] for vector in vectors]
+    packed = pack_shard(w_query, w_key, w_value, w_out, w_inner, w_outer, vectors)
+    gathered = lax.all_gather(packed, "batch", axis=0)
+
+    def weight(at, count):
+        return gathered[:, at : at + count].reshape(-1, width)
+
+    squares = [weight(i * part, part) for i in range(4 + chunks)]
+    outer_at = (4 + chunks) * part
+    w_outer_all = weight(outer_at, outer_part)
+    small = gathered[:, outer_at + outer_part :].reshape(gathered.shape[0], -1)
+    vec = jnp.concatenate(vec_table(small, sizes)).reshape(-1, width).astype(f32)
+    vec = jnp.concatenate([vec, jnp.zeros((16 - vec.shape[0], width), f32)])
+    return jnp.concatenate(squares[:3], 1), squares[3], jnp.concatenate(squares[4:], 1), w_outer_all, vec
 
 
 def body(
@@ -356,33 +761,32 @@
     vectors = (b_query, b_value, b_out, gain_first, bias_first, b_outer, gain_second, bias_second, b_inner)
     sizes = [vector.shape[0] for vector in vectors]
 
-    packed = pack_shard(w_query, w_key, w_value, w_out, w_inner, w_outer, vectors)
-    shard_rows = packed.shape[0]
-    gathered = lax.all_gather(packed, "batch", axis=0)
+    devices = lax.axis_size("batch")
     chunks = inner // width
-
-    def weight(at, count):
-        return gathered[:, at : at + count].reshape(-1, width)
-
-    squares = [weight(i * part, part) for i in range(4 + chunks)]
-    w_qkv = jnp.concatenate(squares[:3], 1)
-    w_out_all = squares[3]
-    w_inner_all = jnp.concatenate(squares[4:], 1)
+    swap = functools.partial(lax.all_to_all, axis_name="blk", tiled=True)
     outer_at = (4 + chunks) * part
-    w_outer_all = weight(outer_at, outer_part)
-    small = gathered[:, outer_at + outer_part :].reshape(gathered.shape[0], -1)
-    vec = jnp.concatenate(vec_table(small, sizes)).reshape(-1, width).astype(f32)
-    vec = jnp.concatenate([vec, jnp.zeros((16 - vec.shape[0], width), f32)])
-
-    masked = cotangent * span_mask[..., None].astype(bf16)
-    swap = functools.partial(lax.all_to_all, axis_name="blk", tiled=True)
-    x = swap(tokens, split_axis=0, concat_axis=1)
-    cot = swap(masked, split_axis=0, concat_axis=1)
-
-    q, k, v, cb, stat_l = attention_call(x, w_qkv, vec)
-    out, mid, gf, ga, gc, stat_d, hidden, gu, sums_ffn = feed_forward_call(
-        x, cb, cot, w_out_all, w_inner_all, w_outer_all, vec
-    )
+    shard_rows = -(-(outer_at + outer_part + 1) // 16) * 16
+    if (devices, lax.axis_size("blk")) == (16, 2):
+        table = sum(
+            lax.pad(
+                vector.astype(f32).reshape(1, -1), f32(0), ((i, 15 - i, 0), (0, width - vector.shape[0], 0))
+            )
+            for i, vector in enumerate(vectors)
+        )
+        x, q, k, v, cb, stat_l, out, mid, gf, ga, gc, stat_d, hidden, gu, sums_ffn, w_qkv = forward_call(
+            tokens, span_mask, cotangent, w_query, w_key, w_value, w_out, w_inner, w_outer, table, (4, 2, 2)
+        )
+    else:
+        w_qkv, w_out_all, w_inner_all, w_outer_all, vec = gather_weights(
+            w_query, w_key, w_value, w_out, w_inner, w_outer, vectors
+        )
+        masked = cotangent * span_mask[..., None].astype(bf16)
+        x = swap(tokens, split_axis=0, concat_axis=1)
+        cot = swap(masked, split_axis=0, concat_axis=1)
+        q, k, v, cb, stat_l = attention_call(x, w_qkv, vec)
+        out, mid, gf, ga, gc, stat_d, hidden, gu, sums_ffn = feed_forward_call(
+            x, cb, cot, w_out_all, w_inner_all, w_outer_all, vec
+        )
     gx, gw_qkv, sums_att = attention_back_call(x, q, k, v, gc, ga, stat_l, stat_d, w_qkv)
     output = swap(out, split_axis=1, concat_axis=0)
     grad_tokens = swap(gx, split_axis=1, concat_axis=0)
@@ -394,7 +798,6 @@
     gw_inner = weight_grad_call(flat(mid), flat(gu), False)
     gw_outer = weight_grad_call(flat(hidden), flat(gf), True)
 
-    devices = gathered.shape[0]
     sums = sums_ffn + sums_att
     small_sums = [sums[i].reshape(devices, -1) for i in range(B_INNER)]
     small_sums.append(sums[B_INNER : B_INNER + chunks].reshape(devices, -1))

time: 611 us -> 513 us (0.84)
  waiting for transfers between devices: 255 us -> 158 us
  Pallas kernels: 198 us -> 262 us
  local copies, waits for them, and re-layouts: 104 us -> 58.5 us
  other arithmetic: 14 us -> 3.07 us
  starting transfers between devices: 18.9 us -> 9.5 us
    all_to_all x2 -> x0, waiting for transfers between devices: 67.4 us -> none  [the longest x1 34 us: body(): cot = swap(masked, split_axis=0, concat_axis=1)]
    pallas_call x2 -> x1, Pallas kernels: 103 us -> 167 us  [forward_call(): pl.pallas_call(kernel, in_specs=[hbm, whole_vmem()] + [hbm] * 7 + [whole_...]
    all_to_all x1, waiting for transfers between devices: 0.01 us -> 30.9 us  [body(): output = swap(out, split_axis=1, concat_axis=0)]
    all_to_all x1, waiting for transfers between devices: 30.3 us -> 0.01 us  [body(): grad_tokens = swap(gx, split_axis=1, concat_axis=0)]
    all_gather x1 -> x0, waiting for transfers between devices: 29.5 us -> none  [body(): gathered = lax.all_gather(packed, 'batch', axis=0)]
    unnamed x48 -> x24, local copies, waits for them, and re-layouts: 36.9 us -> 16.3 us
    slice x5 -> x0, local copies, waits for them, and re-layouts: 13 us -> none  [the longest x2 11.3 us: weight(): return gathered[:, at:at + count].reshape(-1, width)]
    all_to_all x2 -> x0, starting transfers between devices: 9.44 us -> none  [the longest x1 5.22 us: body(): cot = swap(masked, split_axis=0, concat_axis=1)]
  transfers between devices with their start and end apart: 7 -> 4, of which waited for: 6 -> 3; matrix products, arithmetic and copies ran while one was open for 4% -> 3% of each run, Pallas kernels for 0% -> 0%
where the time goes in v2:
time: 513 us; the launch traced here: 506 us
  Pallas kernels  262 us (51%)
  waiting for transfers between devices  158 us (31%)
  local copies, waits for them, and re-layouts  58.5 us (11%)
  between operations  14.6 us (3%)
  starting transfers between devices  9.5 us (2%)
    pallas_call x1, Pallas kernels, forward_call(): pl.pallas_call(kernel, in_specs=[hbm, whole_vmem()] + [hbm] * 7 + [whole_...  167 us
    reduce_scatter x1, waiting for transfers between devices, body(): share = lax.psum_scatter(grads, 'batch', scatter_dimension=0, tiled=False)  95.1 us
    pallas_call x1, Pallas kernels, attention_back_call(): pl.pallas_call(kernel, grid=(count,), in_specs=[spec(block)] * 6 + [spec(...  59 us
    pallas_call x3, Pallas kernels, weight_grad_call(): pl.pallas_call(kernel, grid=(grid,), in_specs=[pl.BlockSpec((tokens, step...  35.9 us
    psum x1, waiting for transfers between devices, body(): share = lax.psum(share, 'blk').astype(f32)  32.5 us
    all_to_all x1, waiting for transfers between devices, body(): output = swap(out, split_axis=1, concat_axis=0)  30.9 us
    unnamed x24, local copies, waits for them, and re-layouts  16.3 us
  transfers between devices with their start and end apart: 4, of which 3 were waited for; matrix products, arithmetic and copies ran while one was open for 3% of the time, Pallas kernels for 0%

profile of v2, /device:TPU:0, one launch (start us, length us, event | category | flops | bytes accessed | tf_op | source)
XLA Modules:
  0.0 505.9 jit_solution(65149099146302881)
XLA Ops:
  7.2 0.7 reshape.133
  7.9 1.4 convert_add_fusion.table_in
  9.3 166.9 %forward.1 = (bf16[4,512,768]{2,1,0:T(8,128)(2,1)}, bf16[4,512,768]{2,1,0:T(8,128)(2,1)}, bf16[4,512,768]{2,1,0:T(8,128)(2,1)}, bf16[4,512,768]{2,1,0:T(8,128)(2...) custom-call(bf16[8,256,768]{2,1,0:T(8,128)(2,1)} %tokens_ref.1, ...), custom_call_target="tpu_custom_call" | custom-call | tf_op jit(solution)/shard_map/forward/pallas_call | solution.py:670
  176.2 59.0 %attention_back.1 = (bf16[4,512,768]{2,1,0:T(8,128)(2,1)}, bf16[768,2304]{1,0:T(8,128)(2,1)}, f32[16,768]{1,0:T(8,128)}) custom-call(bf16[4,512,768]{2,1,0:T(8,128)(2,1)} %get-tuple-element.37.x_ref, bf16[4,512,768]{2,1,0:T(8,128)(2,1)} %get-tuple-element.38.q_ref, bf16[4,512,768]{2,1,0:T(8,128)(2,1)} %get-tuple-element.39.k_ref, ...), custom_call_target="tpu_custom_call" | custom-call | tf_op jit(solution)/shard_map/attention_back/pallas_call | solution.py:299
  235.2 0.8 add_convert_fusion
  236.1 0.7 slice_reduce_fusion
  236.8 14.8 %weight_grad.4 = bf16[768,3072]{1,0:T(8,128)(2,1)} custom-call(bf16[2048,768]{1,0:T(8,128)(2,1)} %bitcast.51, bf16[2048,3072]{1,0:T(8,128)(2,1)} %bitcast.38), custom_call_target="tpu_custom_call" | custom-call | tf_op jit(solution)/shard_map/weight_grad/pallas_call | solution.py:260
  251.6 3.7 fusion
  255.3 0.7 reshape_squeeze.39
  255.9 0.1 reshape.149
  256.0 0.8 reshape_squeeze.38
  256.8 0.8 reshape_squeeze.37
  257.6 1.4 reshape_squeeze.36
  258.9 1.4 reshape_squeeze.35
  260.3 1.3 reshape_squeeze.34
  261.6 1.3 reshape_squeeze.33
  262.9 1.4 reshape_squeeze.32
  264.3 1.5 concatenate.10
  265.8 0.8 pad.76
  266.6 3.6 fusion.1
  270.2 1.1 constant_dynamic-update-slice_fusion.9
  271.3 6.5 %weight_grad.3 = bf16[768,768]{1,0:T(8,128)(2,1)} custom-call(bf16[2048,768]{1,0:T(8,128)(2,1)} %bitcast.50, bf16[2048,768]{1,0:T(8,128)(2,1)} %bitcast.40), custom_call_target="tpu_custom_call" | custom-call | tf_op jit(solution)/shard_map/weight_grad/pallas_call | solution.py:260
  277.8 14.6 %weight_grad.5 = bf16[3072,768]{1,0:T(8,128)(2,1)} custom-call(bf16[2048,3072]{1,0:T(8,128)(2,1)} %bitcast.37, bf16[2048,768]{1,0:T(8,128)(2,1)} %bitcast.49), custom_call_target="tpu_custom_call" | custom-call | tf_op jit(solution)/shard_map/weight_grad/pallas_call | solution.py:260
  292.4 2.6 constant_dynamic-update-slice_fusion.8
  295.0 1.2 constant_dynamic-update-slice_fusion.7
  296.2 2.4 constant_dynamic-update-slice_fusion.6
  298.6 1.1 constant_dynamic-update-slice_fusion.5
  299.7 1.1 constant_dynamic-update-slice_fusion.4
  300.8 1.1 constant_dynamic-update-slice_fusion.3
  301.9 1.1 constant_dynamic-update-slice_fusion.2
  303.1 2.6 constant_dynamic-update-slice_fusion.1
  305.7 0.8 constant_dynamic-update-slice_fusion
  306.5 1.9 copy-done.3
  308.4 4.1 copy.37
  312.5 4.2 all-to-all-start
  316.7 6.5 %copy.39 = bf16[4,512,768]{2,0,1:T(4,128)(2,1)} copy(bf16[4,512,768]{2,1,0:T(8,128)(2,1)} %get-tuple-element.46) | data formatting | bytes 6291456 | tf_op jit(solution)/shard_map/attention_back/pallas_call | solution.py:299
  323.1 30.9 %all-to-all-done = bf16[4,512,768]{2,0,1:T(4,128)(2,1)S(1)} async-done(((bf16[4,512,768]{2,0,1:T(4,128)(2,1)}), bf16[4,512,768]{2,0,1:T(4,128)(2,1)S(1)}, u32[]{:S(2)}, u32[]{:S(2)}) %all-to-all-start) | async-done | bytes 3145760 | tf_op jit(solution)/shard_map/all_to_all | solution.py:791
  354.0 5.2 %all-to-all-start.1 = ((bf16[4,512,768]{2,0,1:T(4,128)(2,1)}), bf16[4,512,768]{2,0,1:T(4,128)(2,1)}, u32[]{:S(2)}, u32[]{:S(2)}) async-start(bf16[4,512,768]{2,0,1:T(4,128)(2,1)} %copy.39), calls=%async_computation.1 | async-start | bytes 6291456 | tf_op jit(solution)/shard_map/all_to_all | solution.py:792
  359.3 95.1 %reduce-scatter.2.cloned.1.call-done = bf16[1,592,768]{2,1,0:T(8,128)(2,1)} async-done(((bf16[16,592,768]{2,1,0:T(8,128)(2,1)}), bf16[1,592,768]{2,1,0:T(8,128)(2,1)}) %reduce-scatter.2.cloned.1.call-update) | async-done | bytes 909328 | tf_op jit(solution)/shard_map/reduce_scatter | solution.py:812
  454.4 2.1 copy.38
  456.5 4.0 copy.40
  460.4 32.5 %all-reduce.12.cloned.1.call-done = bf16[592,768]{1,0:T(8,128)(2,1)} async-done(((bf16[592,768]{1,0:T(8,128)(2,1)}), bf16[592,768]{1,0:T(8,128)(2,1)}) %all-reduce.12.cloned.1.call-update) | async-done | bytes 909328 | tf_op jit(solution)/shard_map/psum | solution.py:813
  492.9 0.8 slice.163
  493.8 0.6 slice.176
  494.3 0.6 fusion.3
  494.9 2.0 fusion.2
  496.9 0.9 pad_maximum_fusion
  497.8 0.9 slice.177
  (22 shorter events, 0.2 us)
Async XLA Ops:
  7.2 447.2 %reduce-scatter.2.cloned.1.call-start = ((), (), s32[]{:S(2)}) async-start(), calls=%async_computation.3 | async-start | bytes 15458304 | tf_op jit(solution)/shard_map/reduce_scatter | solution.py:812
  176.2 59.0 %copy-start.4 = (f32[16,768]{1,0:T(8,128)S(1)}, f32[16,768]{1,0:T(8,128)}, u32[]{:S(2)}) copy-start(f32[16,768]{1,0:T(8,128)} %get-tuple-element.53) | copy-start | bytes 147460
  292.4 2.6 copy-start.1
  292.4 6.2 %copy-start = (bf16[768,768]{1,0:T(8,128)(2,1)S(1)}, bf16[768,768]{1,0:T(8,128)(2,1)}, u32[]{:S(2)}) copy-start(bf16[768,768]{1,0:T(8,128)(2,1)} %get-tuple-element.66) | copy-start | bytes 3538948
  292.4 10.6 %slice-start = ((s8[4718592]{0:T(1024)(128)(4,1)}), s8[4194304]{0:T(1024)(128)(4,1)S(1)}, s32[]{:S(2)}) async-start(s8[4718592]{0:T(1024)(128)(4,1)} %bitcast.34), calls=%async_computation.5 | async-start | bytes 8388608
  298.6 4.5 slice-start.1
  306.5 1.9 copy-start.3
  312.5 41.6 %all-to-all-start = ((bf16[4,512,768]{2,0,1:T(4,128)(2,1)}), bf16[4,512,768]{2,0,1:T(4,128)(2,1)S(1)}, u32[]{:S(2)}, u32[]{:S(2)}) async-start(bf16[4,512,768]{2,0,1:T(4,128)(2,1)} %copy.37), calls=%async_computation | async-start | bytes 6291456 | tf_op jit(solution)/shard_map/all_to_all | solution.py:791
  354.0 102.4 %all-to-all-start.1 = ((bf16[4,512,768]{2,0,1:T(4,128)(2,1)}), bf16[4,512,768]{2,0,1:T(4,128)(2,1)}, u32[]{:S(2)}, u32[]{:S(2)}) async-start(bf16[4,512,768]{2,0,1:T(4,128)(2,1)} %copy.39), calls=%async_computation.1 | async-start | bytes 6291456 | tf_op jit(solution)/shard_map/all_to_all | solution.py:792
  359.3 133.7 %all-reduce.12.cloned.1.call-start = ((), (), s32[]{:S(2)}) async-start(), calls=%async_computation.4 | async-start | bytes 1818624 | tf_op jit(solution)/shard_map/psum | solution.py:813
  492.9 4.9 copy-start.2
Sparse Core Ops, SparseCore 0:
  306.7 147.6 reduce-scatter.1
  456.8 36.1 all-reduce.11

commit v3 on v2

--- a/solution.py
+++ b/solution.py
@@ -96,31 +96,30 @@
     l_ref[...] = stat[...].T[:STAT_ROWS]
 
 
-def attend_back(q_ref, k_ref, v_ref, g_ref, l_ref, d_ref, gq_ref, gk_ref, gv_ref, kt, gqt):
-    kt[...] = (k_ref[...] * bf16(HEAD_DIM**-0.5)).T
-
-    def pair(p, carry):
-        at = pair_at(p)
+def attend_back(q_ref, k_ref, v_ref, g_ref, l_ref, d_ref, out_ref, kt, gqt, first, pairs):
+    part = pairs * PAIR
+    columns = pl.ds(pl.multiple_of(first * PAIR, PAIR), part)
+    kt[...] = (k_ref[:, columns] * bf16(HEAD_DIM**-0.5)).T
+    for p in range(pairs):
+        at = pair_at(first + p)
         q2, g2 = q_ref[:, at], g_ref[:, at]
         ks, vs = halves(k_ref[:, at]), halves(v_ref[:, at])
         qs, gs = halves(q2), halves(g2)
         gk = gv = None
         for h in range(2):
-            probs = jnp.exp(mul(ks[h], q2, NT) - l_ref[pl.ds(2 * p + h, 1), :])
+            head = 2 * (first + p) + h
+            probs = jnp.exp(mul(ks[h], q2, NT) - l_ref[pl.ds(head, 1), :])
             grad_probs = mul(vs[h], g2, NT)
-            grad_scores = (probs * (grad_probs - d_ref[pl.ds(2 * p + h, 1), :])).astype(bf16)
+            grad_scores = (probs * (grad_probs - d_ref[pl.ds(head, 1), :])).astype(bf16)
             gk_one = mul(grad_scores, qs[h])
             gv_one = mul(probs.astype(bf16), gs[h])
             gk = gk_one if gk is None else gk + gk_one
             gv = gv_one if gv is None else gv + gv_one
-            rows = pl.ds(pl.multiple_of((2 * p + h) * HEAD_DIM, HEAD_DIM), HEAD_DIM)
+            rows = slice((2 * p + h) * HEAD_DIM, (2 * p + h + 1) * HEAD_DIM)
             gqt[rows, :] = mul(kt[rows, :], grad_scores).astype(bf16)
-        gk_ref[:, at] = gk.astype(bf16)
-        gv_ref[:, at] = gv.astype(bf16)
-        return carry
-
-    lax.fori_loop(0, HEADS // 2, pair, 0, unroll=2)
-    gq_ref[...] = gqt[...].T
+        out_ref[:, part + p * PAIR : part + (p + 1) * PAIR] = gk.astype(bf16)
+        out_ref[:, 2 * part + p * PAIR : 2 * part + (p + 1) * PAIR] = gv.astype(bf16)
+    out_ref[:, :part] = gqt[...].T
 
 
 def feed_forward(
@@ -271,8 +270,9 @@
 def attention_back_call(x, q, k, v, gc, ga, stat_l, stat_d, w_qkv):
     count, length, width = x.shape
     block = (None, length, width)
-
-    def kernel(x_ref, q_ref, k_ref, v_ref, gc_ref, ga_ref, l_ref, d_ref, w_ref, gx_ref, gw_ref, sums_ref, kt, gqt, gq, gk, gv, total):
+    pairs = HEADS // 2
+
+    def kernel(x_ref, q_ref, k_ref, v_ref, gc_ref, ga_ref, l_ref, d_ref, w_ref, gx_ref, gw_ref, sums_ref, kt, gqt, g, total):
         step = pl.program_id(0)
 
         @pl.when(step == 0)
@@ -280,22 +280,21 @@
             sums_ref[...] = jnp.zeros_like(sums_ref)
             total[...] = jnp.zeros_like(total)
 
-        attend_back(q_ref, k_ref, v_ref, gc_ref, l_ref, d_ref, gq, gk, gv, kt, gqt)
-        sums_ref[B_QUERY : B_QUERY + 1, :] += column_sum(gq[...])
-        sums_ref[B_VALUE : B_VALUE + 1, :] += column_sum(gv[...])
+        attend_back(q_ref, k_ref, v_ref, gc_ref, l_ref, d_ref, g, kt, gqt, 0, pairs)
+        sums_ref[B_QUERY : B_QUERY + 1, :] += column_sum(g[:, :width])
+        sums_ref[B_VALUE : B_VALUE + 1, :] += column_sum(g[:, 2 * width :])
         grad = ga_ref[...].astype(f32)
         x = x_ref[...]
-        for i, ref in enumerate((gq, gk, gv)):
+        for i in range(3):
             at = slice(i * width, (i + 1) * width)
-            grad = grad + mul(ref[...], w_ref[:, at], NT)
-            total[:, at] += mul(x, ref[...], TN)
+            grad = grad + mul(g[:, at], w_ref[:, at], NT)
+            total[:, at] += mul(x, g[:, at], TN)
         gx_ref[...] = grad.astype(bf16)
 
         @pl.when(step == count - 1)
         def _():
             gw_ref[...] = total[...].astype(bf16)
 
-    seq_scratch = pltpu.VMEM((length, width), bf16)
     return pl.pallas_call(
         kernel,
         grid=(count,),
@@ -306,7 +305,8 @@
             jax.ShapeDtypeStruct((width, 3 * width), bf16),
             jax.ShapeDtypeStruct((16, width), f32),
         ],
-        scratch_shapes=[pltpu.VMEM((width, length), bf16)] * 2 + [seq_scratch] * 3 + [pltpu.VMEM((width, 3 * width), f32)],
+        scratch_shapes=[pltpu.VMEM((width, length), bf16)] * 2
+        + [pltpu.VMEM((length, 3 * width), bf16), pltpu.VMEM((width, 3 * width), f32)],
         compiler_params=params(),
         name="attention_back",
     )(x, q, k, v, gc, ga, stat_l, stat_d, w_qkv)
@@ -694,6 +694,396 @@
     )(tokens, span_mask, cotangent, w_query, w_key, w_value, w_out, w_inner, w_outer, table)
 
 
+def backward_call(x, q, k, v, cb, mid, gf, ga, gc, hidden, gu, out, stat_l, stat_d, w_qkv, sums, sizes):
+    depth_z, depth_y, cores = sizes
+    count, length, width = x.shape
+    inner = hidden.shape[2]
+    devices = depth_z * depth_y * cores
+    part, outer_part = width // devices, inner // devices
+    stretch, rows = length // 2, 2 * count
+    chunks = inner // width
+    GROUPS = 3
+    pairs = HEADS // 2 // GROUPS
+    column = pairs * PAIR
+    narrow = width // GROUPS
+    OUT = chunks
+    QKV = chunks + 1
+    N = QKV + GROUPS
+    SLOTS = 2
+    STEPS = 5
+    tokens_all = count * length
+
+    def kernel(
+        x_in, q_in, k_in, v_in, cb_in, mid_in, gf_in, ga_in, gc_in, h_in, gu_in, out_in, w_in, l_ref, d_ref, sums_ref,
+        output, grad_tokens, g_query, g_key, g_value, g_out, g_inner, g_outer, vectors,
+        big, pool, w_cat, ga_s, gx_s, kt, gqt, own_s, own_o, r1, r2, r3, s4, r4, r1o, r2o, r3o, s4o, r4o, v_own, v_got,
+        s1_send, s1_recv, s2_send, s2_recv, s3_send, s3_recv, s4_send, s4_recv,
+        v_send, v_recv, o_send, o_recv, g_send, g_recv, big_sem, pool_sem, w_sem, ga_sem, keep_sem,
+    ):
+        b, k = lax.axis_index("batch"), lax.axis_index("blk")
+        z, y, c = b // (depth_y * cores), (b // cores) % depth_y, b % cores
+
+        def at(z_, y_, c_):
+            return (z_ * depth_y + y_) * cores + c_
+
+        beside = (b, 1 - k)
+        other_core = (at(z, y, 1 - c), k)
+        other_y = (at(z, 1 - y, c), k)
+
+        def level(j):
+            return (z + j) % depth_z
+
+        barrier = pltpu.get_barrier_semaphore()
+        partners = [beside, other_core, other_y] + [(at(level(j), y, c), k) for j in range(1, depth_z)]
+        for device in partners:
+            pl.semaphore_signal(barrier, inc=1, device_id=device, device_id_type=pl.DeviceIdType.MESH)
+
+        def remote(src, dst, device, send, recv):
+            return pltpu.make_async_remote_copy(
+                src_ref=src, dst_ref=dst, send_sem=send, recv_sem=recv, device_id=device, device_id_type=pl.DeviceIdType.MESH
+            )
+
+        def load(i, src):
+            return pltpu.make_async_copy(src, big.at[i], big_sem.at[i])
+
+        def wide_load(i, src, j):
+            return pltpu.make_async_copy(src.at[:, :, j * width : (j + 1) * width], big.at[i], big_sem.at[i])
+
+        def pool_load(s, slot):
+            return [
+                pltpu.make_async_copy(src.at[s], pool.at[slot, i], pool_sem.at[slot, i])
+                for i, src in enumerate((q_in, k_in, v_in, gc_in))
+            ]
+
+        def w_load(i, g):
+            return pltpu.make_async_copy(
+                w_in.at[:, i * width + g * column : i * width + (g + 1) * column],
+                w_cat.at[g, :, i * column : (i + 1) * column],
+                w_sem.at[i, g],
+            )
+
+        first_loads = [load(0, mid_in), wide_load(2, gu_in, 0), load(1, gf_in), wide_load(3, gu_in, 1)]
+        for copy in first_loads:
+            copy.start()
+        mine = pl.ds(pl.multiple_of(k * stretch, stretch), stretch)
+        theirs = pl.ds(pl.multiple_of((1 - k) * stretch, stretch), stretch)
+
+        def buffers(g, outer):
+            if outer:
+                return own_o.at[g], r1o.at[g], r2o.at[g], r3o.at[g], s4o.at[g], r4o.at[g], N + g
+            return own_s.at[g % SLOTS], r1.at[g], r2.at[g], r3.at[g], s4.at[g], r4.at[g], g
+
+        def step_1(g, outer=False):
+            own, a1, _, _, _, _, i = buffers(g, outer)
+            return remote(own.at[:, :, 1 - c], a1, other_core, s1_send.at[i], s1_recv.at[i])
+
+        def step_2(g, outer=False):
+            _, a1, a2, _, _, _, i = buffers(g, outer)
+            return remote(a1.at[:, 1 - y], a2, other_y, s2_send.at[i], s2_recv.at[i])
+
+        def step_3(g, j, outer=False):
+            _, _, a2, a3, _, _, i = buffers(g, outer)
+            return remote(
+                a2.at[level(j)], a3.at[j - 1], (at(level(j), y, c), k), s3_send.at[i, j - 1], s3_recv.at[i, j - 1]
+            )
+
+        def step_4(g, outer=False):
+            _, _, _, _, a4, b4, i = buffers(g, outer)
+            return remote(a4, b4, beside, s4_send.at[i], s4_recv.at[i])
+
+        def move_1(g, outer=False):
+            own, a1, _, _, _, _, _ = buffers(g, outer)
+            step_1(g, outer).wait()
+
+            def add(i, carry):
+                zi, yi = i // depth_y, i % depth_y
+                a1[zi, yi] = a1[zi, yi] + own[zi, yi, c]
+                return carry
+
+            lax.fori_loop(0, depth_z * depth_y, add, 0)
+            step_2(g, outer).start()
+
+        def move_2(g, outer=False):
+            _, a1, a2, _, _, _, _ = buffers(g, outer)
+            step_2(g, outer).wait()
+
+            def add(zi, carry):
+                a2[zi] = a2[zi] + a1[zi, y]
+                return carry
+
+            lax.fori_loop(0, depth_z, add, 0)
+            for j in range(1, depth_z):
+                step_3(g, j, outer).start()
+
+        def move_3(g, outer=False):
+            _, _, a2, a3, a4, _, _ = buffers(g, outer)
+            for j in range(1, depth_z):
+                step_3(g, j, outer).wait()
+            total = a2[z].astype(f32)
+            for j in range(1, depth_z):
+                total = total + a3[j - 1].astype(f32)
+            a4[...] = total.astype(bf16)
+            step_4(g, outer).start()
+
+        def move_4(g, outer=False):
+            _, _, _, _, a4, b4, _ = buffers(g, outer)
+            step_4(g, outer).wait()
+            total = a4[...].astype(f32) + b4[...].astype(f32)
+            if outer:
+                g_outer[:, g * narrow : (g + 1) * narrow] = total
+            elif g < OUT:
+                g_inner[:, g * width : (g + 1) * width] = total
+            elif g == OUT:
+                g_out[...] = total
+            else:
+                for i, ref in enumerate((g_query, g_key, g_value)):
+                    ref[:, (g - QKV) * column : (g - QKV + 1) * column] = total[:, i * column : (i + 1) * column]
+
+        def whole(i):
+            return big[i].reshape(tokens_all, width)
+
+        def begin(g, value):
+            own_s[g % SLOTS] = value.astype(bf16).reshape(depth_z, depth_y, cores, part, width)
+            step_1(g).start()
+
+        pl.semaphore_wait(barrier, len(partners))
+        output_copies = [
+            remote(out_in.at[s, theirs], output.at[k * count + s], beside, o_send.at[s], o_recv.at[s]) for s in range(count)
+        ]
+        keep_output = pltpu.make_async_copy(out_in.at[:, mine], output.at[pl.ds(k * count, count)], keep_sem.at[0])
+        for copy in output_copies:
+            copy.start()
+
+        first_loads[0].wait()
+        for j in range(chunks):
+            wide_load(2 + j % 2, gu_in, j).wait()
+            if j >= SLOTS:
+                move_1(j - SLOTS)
+            begin(j, mul(whole(0), whole(2 + j % 2), TN))
+            following = j + 2 - chunks
+            if following < 0:
+                wide_load(2 + j % 2, gu_in, j + 2).start()
+            else:
+                wide_load(2 + j % 2, h_in, following).start()
+            if j == 0:
+                for s in range(2):
+                    for copy in pool_load(s, s):
+                        copy.start()
+            if j == 1:
+                keep_output.start()
+                for g in range(GROUPS):
+                    for i in range(3):
+                        w_load(i, g).start()
+        load(0, ga_in).start()
+        first_loads[2].wait()
+        for j in range(chunks):
+            wide_load(2 + j % 2, h_in, j).wait()
+            product = mul(whole(2 + j % 2), whole(1), TN).astype(bf16)
+            for g in range(GROUPS):
+                own_o[g, j] = product[:, g * narrow : (g + 1) * narrow].reshape(depth_y, cores, outer_part, narrow)
+            if j + 2 < chunks:
+                wide_load(2 + j % 2, h_in, j + 2).start()
+            elif j + 2 == chunks:
+                load(2 + j % 2, cb_in).start()
+            else:
+                load(2 + j % 2, x_in).start()
+            if j < SLOTS:
+                move_1(chunks - SLOTS + j)
+            if j == 2:
+                move_2(0)
+        for g in range(GROUPS):
+            step_1(g, True).start()
+        move_2(1)
+        load(0, ga_in).wait()
+        load(2 + chunks % 2, cb_in).wait()
+        begin(OUT, mul(whole(2 + chunks % 2), whole(0), TN))
+        for copy in pool_load(2, 2):
+            copy.start()
+        move_3(0)
+        for g in range(GROUPS):
+            for i in range(3):
+                w_load(i, g).wait()
+        load(2 + (chunks + 1) % 2, x_in).wait()
+        x_at = 2 + (chunks + 1) % 2
+        v_own[0] = sums_ref[...]
+
+        half = count // 2
+        cells = GROUPS * count
+        plan = {
+            0: [lambda: [move_1(g, True) for g in range(GROUPS)], lambda: move_2(2)],
+            1: [lambda: move_1(OUT), lambda: move_3(1), lambda: move_4(0)],
+            2: [lambda: move_2(3)],
+            3: [lambda: move_3(2), lambda: move_4(1)],
+            4: [lambda: move_2(0, True), lambda: move_3(3), lambda: move_4(2)],
+            5: [lambda: move_4(3)],
+            6: [lambda: move_2(1, True), lambda: move_3(0, True)],
+            7: [lambda: move_4(0, True)],
+            8: [lambda: move_2(2, True), lambda: move_3(1, True), lambda: move_1(QKV)],
+            9: [lambda: move_2(OUT), lambda: move_4(1, True)],
+            10: [lambda: move_3(2, True), lambda: move_2(QKV), lambda: move_1(QKV + 1)],
+            11: [lambda: move_4(2, True), lambda: move_3(OUT)],
+        }
+
+        def pick(i):
+            late = i // (GROUPS * half)
+            j = i % (GROUPS * half)
+            s = (1 - late) * (j // GROUPS) + late * (half + j % half)
+            g = (1 - late) * (j % GROUPS) + late * (j // half)
+            return s, g
+
+        def gx_copies(s):
+            away = remote(gx_s.at[theirs], grad_tokens.at[k * count + s], beside, g_send.at[s], g_recv.at[s])
+            keep = pltpu.make_async_copy(gx_s.at[mine], grad_tokens.at[k * count + s], keep_sem.at[1])
+            return away, keep
+
+        ga_load = [pltpu.make_async_copy(ga_in.at[s], ga_s, ga_sem.at[0]) for s in range(count)]
+        ga_load[0].start()
+
+        def cell(i, carry):
+            s, g = pick(i)
+            slot = s % 3
+
+            @pl.when(g == 0)
+            def _():
+                for copy in pool_load(s, slot):
+                    copy.wait()
+
+            attend_back(
+                pool.at[slot, 0], pool.at[slot, 1], pool.at[slot, 2], pool.at[slot, 3], l_ref.at[s], d_ref.at[s],
+                big.at[g, s], kt, gqt, g * pairs, pairs,
+            )
+            span = pl.ds(pl.multiple_of(g * column, column), column)
+            v_own[0, B_QUERY : B_QUERY + 1, span] += column_sum(big[g, s, :, :column])
+            v_own[0, B_VALUE : B_VALUE + 1, span] += column_sum(big[g, s, :, 2 * column :])
+
+            @pl.when(i == GROUPS - 1)
+            def _():
+                for copy in pool_load(3, 0):
+                    copy.start()
+
+            for when, steps in plan.items():
+                @pl.when(i == when)
+                def _():
+                    for step in steps:
+                        step()
+
+            late = i // (GROUPS * half)
+
+            @pl.when((late == 1) & (i % half == half - 1))
+            def _():
+                begin(QKV + g, mul(whole(x_at), big[g].reshape(tokens_all, width), TN))
+
+            @pl.when(g == GROUPS - 1)
+            def _():
+                ga_load[0].wait()
+
+                @pl.when(s > 0)
+                def _():
+                    away, keep = gx_copies(s - 1)
+                    away.wait_send()
+                    keep.wait()
+
+                grad = ga_s[...].astype(f32)
+                for group in range(GROUPS):
+                    grad = grad + mul(big[group, s], w_cat[group], NT)
+                gx_s[...] = grad.astype(bf16)
+                away, keep = gx_copies(s)
+                away.start()
+                keep.start()
+
+                @pl.when(s < count - 1)
+                def _():
+                    pltpu.make_async_copy(ga_in.at[s + 1], ga_s, ga_sem.at[0]).start()
+
+            return carry
+
+        lax.fori_loop(0, cells, cell, 0)
+
+        towards = [other_core, other_y, (at(z + 1 - 2 * (z % 2), y, c), k), (at((z + 2) % 4, y, c), k), beside]
+
+        def v_copy(i):
+            return remote(v_own.at[i], v_got.at[i], towards[i], v_send.at[i], v_recv.at[i])
+
+        def v_move(i):
+            v_copy(i).wait()
+            v_own[i + 1] = v_own[i] + v_got[i]
+            if i + 1 < STEPS:
+                v_copy(i + 1).start()
+
+        v_copy(0).start()
+        last_group = N - 1
+        move_4(OUT)
+        move_1(last_group)
+        v_move(0)
+        v_move(1)
+        move_3(QKV)
+        v_move(2)
+        move_2(QKV + 1)
+        v_move(3)
+        move_2(last_group)
+        v_move(4)
+        total = v_own[STEPS]
+        inner_row = v_own[STEPS, pl.ds(B_INNER + b // (devices // chunks), 1), :]
+        rolled = pltpu.roll(total, (width - b * part) % width, 1)
+        wide = pltpu.roll(inner_row, (width - (b % (devices // chunks)) * outer_part) % width, 1)
+        line = lax.broadcasted_iota(jnp.int32, total.shape, 0)
+        vectors[...] = jnp.where(line == B_INNER, wide, rolled)
+        move_4(QKV)
+        move_3(QKV + 1)
+        move_3(last_group)
+        move_4(QKV + 1)
+        move_4(last_group)
+        away, keep = gx_copies(count - 1)
+        away.wait_send()
+        keep.wait()
+        keep_output.wait()
+        for s in range(count):
+            output_copies[s].wait_send()
+            remote(out_in.at[s, theirs], output.at[(1 - k) * count + s], beside, o_send.at[s], o_recv.at[s]).wait_recv()
+            remote(gx_s.at[theirs], grad_tokens.at[(1 - k) * count + s], beside, g_send.at[s], g_recv.at[s]).wait_recv()
+
+    hbm = pl.BlockSpec(memory_space=pl.ANY)
+    dma = pltpu.SemaphoreType.DMA
+    every = N + GROUPS
+
+    def vmem(*shape):
+        return pltpu.VMEM(shape, bf16)
+
+    def result(*shape):
+        return jax.ShapeDtypeStruct(shape, f32)
+
+    back = jax.ShapeDtypeStruct((rows, stretch, width), bf16)
+    return pl.pallas_call(
+        kernel,
+        in_specs=[hbm] * 13 + [whole_vmem()] * 3,
+        out_specs=[hbm] * 2 + [whole_vmem()] * 7,
+        out_shape=[
+            back, back, result(part, width), result(part, width), result(part, width), result(part, width),
+            result(part, inner), result(outer_part, width), result(16, width),
+        ],
+        scratch_shapes=[
+            vmem(4, count, length, width),
+            vmem(3, 4, length, width),
+            vmem(GROUPS, width, 3 * column),
+            vmem(length, width), vmem(length, width),
+            vmem(column, length), vmem(column, length),
+            vmem(SLOTS, depth_z, depth_y, cores, part, width),
+            vmem(GROUPS, depth_z, depth_y, cores, outer_part, narrow),
+            vmem(N, depth_z, depth_y, part, width), vmem(N, depth_z, part, width), vmem(N, depth_z - 1, part, width),
+            vmem(N, part, width), vmem(N, part, width),
+            vmem(GROUPS, depth_z, depth_y, outer_part, narrow), vmem(GROUPS, depth_z, outer_part, narrow),
+            vmem(GROUPS, depth_z - 1, outer_part, narrow), vmem(GROUPS, outer_part, narrow), vmem(GROUPS, outer_part, narrow),
+            pltpu.VMEM((STEPS + 1, 16, width), f32), pltpu.VMEM((STEPS, 16, width), f32),
+            dma((every,)), dma((every,)), dma((every,)), dma((every,)),
+            dma((every, depth_z - 1)), dma((every, depth_z - 1)), dma((every,)), dma((every,)),
+            dma((STEPS,)), dma((STEPS,)), dma((count,)), dma((count,)), dma((count,)), dma((count,)),
+            dma((4,)), dma((3, 4)), dma((3, GROUPS)), dma((1,)), dma((2,)),
+        ],
+        compiler_params=pltpu.CompilerParams(collective_id=2, has_side_effects=True, vmem_limit_bytes=63 * 2**20),
+        name="backward",
+    )(x, q, k, v, cb, mid, gf, ga, gc, hidden, gu, out, w_qkv, stat_l, stat_d, sums)
+
+
 def pack_shard(w_query, w_key, w_value, w_out, w_inner, w_outer, vectors):
     width = w_query.shape[1]
     inner_parts = [w_inner[:, i : i + width] for i in range(0, w_inner.shape[1], width)]
@@ -776,17 +1166,25 @@
         x, q, k, v, cb, stat_l, out, mid, gf, ga, gc, stat_d, hidden, gu, sums_ffn, w_qkv = forward_call(
             tokens, span_mask, cotangent, w_query, w_key, w_value, w_out, w_inner, w_outer, table, (4, 2, 2)
         )
-    else:
-        w_qkv, w_out_all, w_inner_all, w_outer_all, vec = gather_weights(
-            w_query, w_key, w_value, w_out, w_inner, w_outer, vectors
+        results = backward_call(
+            x, q, k, v, cb, mid, gf, ga, gc, hidden, gu, out, stat_l, stat_d, w_qkv, sums_ffn, (4, 2, 2)
         )
-        masked = cotangent * span_mask[..., None].astype(bf16)
-        x = swap(tokens, split_axis=0, concat_axis=1)
-        cot = swap(masked, split_axis=0, concat_axis=1)
-        q, k, v, cb, stat_l = attention_call(x, w_qkv, vec)
-        out, mid, gf, ga, gc, stat_d, hidden, gu, sums_ffn = feed_forward_call(
-            x, cb, cot, w_out_all, w_inner_all, w_outer_all, vec
+        output, grad_tokens, g_query, g_key, g_value, g_out, g_inner, g_outer, totals = results
+        small = [totals[i, :size] for i, size in enumerate(sizes)]
+        return (
+            output, grad_tokens, g_query, small[0], g_key, g_value, small[1], g_out, small[2], small[3], small[4], g_inner,
+            small[8], g_outer, small[5], small[6], small[7],
         )
+    w_qkv, w_out_all, w_inner_all, w_outer_all, vec = gather_weights(
+        w_query, w_key, w_value, w_out, w_inner, w_outer, vectors
+    )
+    masked = cotangent * span_mask[..., None].astype(bf16)
+    x = swap(tokens, split_axis=0, concat_axis=1)
+    cot = swap(masked, split_axis=0, concat_axis=1)
+    q, k, v, cb, stat_l = attention_call(x, w_qkv, vec)
+    out, mid, gf, ga, gc, stat_d, hidden, gu, sums_ffn = feed_forward_call(
+        x, cb, cot, w_out_all, w_inner_all, w_outer_all, vec
+    )
     gx, gw_qkv, sums_att = attention_back_call(x, q, k, v, gc, ga, stat_l, stat_d, w_qkv)
     output = swap(out, split_axis=1, concat_axis=0)
     grad_tokens = swap(gx, split_axis=1, concat_axis=0)

time: 513 us -> 336 us (0.65)
  waiting for transfers between devices: 158 us -> 0 us
  Pallas kernels: 262 us -> 315 us
  local copies, waits for them, and re-layouts: 58.5 us -> 13.3 us
  between operations: 14.6 us -> 0.98 us
  starting transfers between devices: 9.5 us -> 0 us
    reduce_scatter x1 -> x0, waiting for transfers between devices: 95.1 us -> none  [body(): share = lax.psum_scatter(grads, 'batch', scatter_dimension=0, tiled=False)]
    pallas_call x4 -> x1, Pallas kernels: 94.9 us -> 148 us  [backward_call(): pl.pallas_call(kernel, in_specs=[hbm] * 13 + [whole_vmem()] * 3, out_spec...]
    psum x1 -> x0, waiting for transfers between devices: 32.5 us -> none  [body(): share = lax.psum(share, 'blk').astype(f32)]
    all_to_all x2 -> x0, waiting for transfers between devices: 30.9 us -> none  [the longest x1 30.9 us: body(): output = swap(out, split_axis=1, concat_axis=0)]
    slice x9 -> x1, local copies, waits for them, and re-layouts: 12.9 us -> 1.26 us  [body(): small = [totals[i, :size] for i, size in enumerate(sizes)]]
    pallas_call x2 -> x0, local copies, waits for them, and re-layouts: 10.5 us -> none  [the longest x1 6.45 us: attention_back_call(): pl.pallas_call(kernel, grid=(count,), in_specs=[spec(block)] * 6 + [spec(...]
    all_to_all x2 -> x0, starting transfers between devices: 9.42 us -> none  [the longest x1 5.22 us: body(): grad_tokens = swap(gx, split_axis=1, concat_axis=0)]
    another operation x8 -> x0, local copies, waits for them, and re-layouts: 8.96 us -> none  [body(): small_sums = [sums[i].reshape(devices, -1) for i in range(B_INNER)]]
  transfers between devices with their start and end apart: 4 -> 0, of which waited for: 3 -> 0; matrix products, arithmetic and copies ran while one was open for 3% -> 0% of each run, Pallas kernels for 0% -> 0%
where the time goes in v3:
time: 336 us; the launch traced here: 331 us
  Pallas kernels  315 us (94%)
  local copies, waits for them, and re-layouts  13.3 us (4%)
    pallas_call x1, Pallas kernels, forward_call(): pl.pallas_call(kernel, in_specs=[hbm, whole_vmem()] + [hbm] * 7 + [whole_...  167 us
    pallas_call x1, Pallas kernels, backward_call(): pl.pallas_call(kernel, in_specs=[hbm] * 13 + [whole_vmem()] * 3, out_spec...  148 us
    unnamed x22, local copies, waits for them, and re-layouts  9.87 us

profile of v3, /device:TPU:0, one launch (start us, length us, event | category | flops | bytes accessed | tf_op | source)
XLA Modules:
  0.0 330.8 jit_solution(1736025286980863882)
XLA Ops:
  0.7 0.7 reshape.78
  1.3 1.4 convert_add_fusion.table_in
  2.7 167.2 %forward.1 = (bf16[4,512,768]{2,1,0:T(8,128)(2,1)}, bf16[4,512,768]{2,1,0:T(8,128)(2,1)}, bf16[4,512,768]{2,1,0:T(8,128)(2,1)}, bf16[4,512,768]{2,1,0:T(8,128)(2...) custom-call(bf16[8,256,768]{2,1,0:T(8,128)(2,1)} %tokens_ref.1, ...), custom_call_target="tpu_custom_call" | custom-call | tf_op jit(solution)/shard_map/forward/pallas_call | solution.py:670
  170.0 147.8 %backward.1 = (bf16[8,256,768]{2,1,0:T(8,128)(2,1)}, bf16[8,256,768]{2,1,0:T(8,128)(2,1)}, f32[48,768]{1,0:T(8,128)}, f32[48,768]{1,0:T(8,128)}, f32[48,768]{1,0...) custom-call(bf16[4,512,768]{2,1,0:T(8,128)(2,1)} %get-tuple-element.42.x_in, ...), custom_call_target="tpu_custom_call" | custom-call | tf_op jit(solution)/shard_map/backward/pallas_call | solution.py:1056
  317.8 1.3 slice.32
  319.1 1.5 slice_bitcast_fusion
  320.6 0.0 copy-start
  320.6 3.9 %copy.43 = bf16[8,256,768]{2,1,0:T(8,128)(2,1)} copy(bf16[8,256,768]{2,1,0:T(8,128)(2,1)} %get-tuple-element.92) | data formatting | bytes 6291456
  324.5 0.0 copy-done
  324.5 0.0 copy-start.6
  324.5 0.0 copy-start.5
  324.5 0.0 copy-start.4
  324.5 0.0 copy-start.3
  324.5 0.0 copy-start.2
  324.5 0.0 copy-start.1
  324.5 1.7 copy.44
  326.2 0.0 copy-done.6
  326.2 0.7 copy.45
  326.9 0.0 copy-done.5
  326.9 0.7 copy.46
  327.5 0.0 copy-done.4
  327.5 0.7 copy.47
  328.2 0.0 copy-done.3
  328.2 0.7 copy.48
  328.8 0.0 copy-done.2
  328.9 0.8 copy.49
  329.7 0.0 copy-done.1
  329.7 0.8 copy.50
Async XLA Ops:
  320.6 3.9 %copy-start = (bf16[8,256,768]{2,1,0:T(8,128)(2,1)S(1)}, bf16[8,256,768]{2,1,0:T(8,128)(2,1)}, u32[]{:S(2)}) copy-start(bf16[8,256,768]{2,1,0:T(8,128)(2,1)} %get-tuple-element.93) | copy-start | bytes 9437188
  324.5 1.7 copy-start.6
  324.5 2.4 copy-start.5
  324.5 3.0 copy-start.4
  324.5 3.7 %copy-start.3 = (f32[48,768]{1,0:T(8,128)S(1)}, f32[48,768]{1,0:T(8,128)}, u32[]{:S(2)}) copy-start(f32[48,768]{1,0:T(8,128)} %get-tuple-element.99) | copy-start | bytes 442372
  324.5 4.3 %copy-start.2 = (f32[48,3072]{1,0:T(8,128)S(1)}, f32[48,3072]{1,0:T(8,128)}, u32[]{:S(2)}) copy-start(f32[48,3072]{1,0:T(8,128)} %get-tuple-element.103) | copy-start | bytes 1769476
  324.5 5.2 %copy-start.1 = (f32[192,768]{1,0:T(8,128)S(1)}, f32[192,768]{1,0:T(8,128)}, u32[]{:S(2)}) copy-start(f32[192,768]{1,0:T(8,128)} %get-tuple-element.105) | copy-start | bytes 1769476
